TPU v7x, 256 devices: a whole 4x4x8 slice. The times are simulated.
256 devices in a mesh: rows: 64 (over z, y, core), grp: 4 (over x).
Axes of the slice: x: 4, y: 4, z: 8, core: 2. Of those that a mesh axis runs over, the one named last changes fastest.
Arguments:
- tiles: bfloat16 [64, 4, 48, 128, 128], P('rows', 'grp'), may hold values from -0.15625 to 0.15625
- tile_row: int32 [64, 4, 48], P('rows', 'grp'), may hold values from 0 to 7
- tile_slot: int32 [64, 4, 48], P('rows', 'grp'), may hold values from 0 to 63
- tile_count: int32 [64, 4], P('rows', 'grp'), may hold values from 6 to 48, as said below
- want: int32 [64, 64], P('rows'), may hold values from 0 to 7
- omega: bfloat16 [65536, 256], P(('rows', 'grp')), may hold values from -6 to 6
Outputs:
- basis: float32 [65536, 256], P(('rows', 'grp'))
- factor: float32 [256, 256], replicated
Inputs may be any that keep to these rules, and one draw needn't show every extreme that they name: `tile_count`: some device has exactly 48 live slots in every draw; every device has 6, 12, 24 or 48.
All inputs are finite; a program needn't handle non-finite values.
Results may differ from a plain program's by a relative error of at most 0.0028.
Values may be sent and summed in bfloat16 or wider, within the bound.
A program may use at most 64 MiB of HBM per device.

v0:
```python
import math

import jax
import jax.numpy as jnp
from jax import lax
from jax.sharding import PartitionSpec as P

RBD = 8


def reduce_group(partial_sum, columns):
    flattened = partial_sum.reshape(-1, columns)
    summed = lax.psum(flattened, "grp").astype(jnp.bfloat16)
    return summed.reshape(partial_sum.shape)


def per_device(tiles, tile_row, tile_slot, tile_count, want, omega):
    tile_size = tiles.shape[-1]
    slot_total = tiles.shape[2]
    columns = omega.shape[1]
    owners = lax.axis_size("rows")
    highest = lax.Precision.HIGHEST
    tiles_here = tiles.reshape(slot_total, tile_size, tile_size)
    row_ids = tile_row.reshape(slot_total)
    slot_ids = tile_slot.reshape(slot_total)
    is_live = jnp.arange(slot_total, dtype=jnp.int32) < tile_count.reshape(())
    live_weight = is_live.astype(jnp.float32)[:, None, None]
    omega_local = lax.all_gather(omega, "grp", axis=0, tiled=True).reshape(RBD, tile_size, columns)
    requests = lax.all_to_all(
        want.reshape(owners, 1), "rows", split_axis=0, concat_axis=0, tiled=True
    ).reshape(owners)

    def forward(ghost_blocks):
        product = jnp.einsum(
            "tab,tbk->tak", tiles_here, ghost_blocks[slot_ids], preferred_element_type=jnp.float32
        )
        return jax.ops.segment_sum(product * live_weight, row_ids, num_segments=RBD)

    ghosts = lax.all_to_all(omega_local[requests], "rows", split_axis=0, concat_axis=0, tiled=True)
    z_full = reduce_group(forward(ghosts), columns)
    product_back = jnp.einsum(
        "tba,tbk->tak", tiles_here, z_full[row_ids], preferred_element_type=jnp.float32
    )
    outgoing = jax.ops.segment_sum(product_back * live_weight, slot_ids, num_segments=owners)
    returned = lax.all_to_all(outgoing, "rows", split_axis=0, concat_axis=0, tiled=True)
    w_part = jax.ops.segment_sum(returned, requests, num_segments=RBD)
    w_full = reduce_group(w_part, columns)
    ghosts_w = lax.all_to_all(w_full[requests], "rows", split_axis=0, concat_axis=0, tiled=True)
    y_part = forward(ghosts_w)
    y_local = lax.psum_scatter(y_part.reshape(-1, columns), "grp", scatter_dimension=0, tiled=True)
    partial_value = jnp.dot(
        y_local.T, y_local, precision=highest, preferred_element_type=jnp.float32
    )
    gram_sum = lax.psum(partial_value, ("rows", "grp"))
    factor_low = jnp.linalg.cholesky(gram_sum)
    norm_scale = math.sqrt(owners * RBD * tile_size)
    basis_out = (
        lax.linalg.triangular_solve(
            factor_low, y_local, left_side=False, lower=True, transpose_a=True
        )
        * norm_scale
    )
    return (basis_out, factor_low.T / norm_scale)


def solution(mesh):
    return jax.shard_map(
        per_device,
        mesh=mesh,
        in_specs=(
            P("rows", "grp", None, None, None),
            P("rows", "grp", None),
            P("rows", "grp", None),
            P("rows", "grp"),
            P("rows", None),
            P(("rows", "grp"), None),
        ),
        out_specs=(P(("rows", "grp"), None), P()),
        check_vma=False,
    )
```

profile of v0, /device:TPU:1, one launch (start us, length us, event | category | flops | bytes accessed | tf_op | source)
XLA Modules:
  0.0 957.6 jit_solution(17952166343164148006)
XLA Ops:
  7.2 0.0 copy-start
  7.2 1.5 copy.36
  8.7 13.2 %all-to-all-start = ((s32[64,1,1]{2,1,0:T(1,128)}), s32[64,1,1]{2,1,0:T(1,128)S(1)}, u32[]{:S(2)}, u32[]{:S(2)}) async-start(s32[64,1,1]{2,1,0:T(1,128)} %copy.36), calls=%async_computation | async-start | bytes 65536 | tf_op jit(solution)/shard_map/all_to_all | solution.py:29
  21.8 11.3 %all_gather.3 = bf16[1024,256]{1,0:T(8,128)(2,1)S(1)} all-gather(bf16[256,256]{1,0:T(8,128)(2,1)} %param.11), channel_id=1, replica_groups=mesh['rows'=64,'grp'=4] {'grp'}, dimensions={0}, use_global_device_ids=true | all-gather | bytes 655360 | tf_op jit(solution)/shard_map/all_gather | solution.py:28
  33.1 0.0 all-to-all-done
  33.1 1.2 reduce.12
  34.3 2.8 gather_fusion
  37.1 12.7 %all-to-all-start.1 = ((bf16[64,128,256]{2,1,0:T(8,128)(2,1)}), bf16[64,128,256]{2,1,0:T(8,128)(2,1)}, u32[]{:S(2)}, u32[]{:S(2)}) async-start(bf16[64,128,256]{2,1,0:T(8,128)(2,1)} %gather_fusion), calls=%async_computation.1 | async-start | bytes 8388608 | tf_op jit(solution)/shard_map/all_to_all | solution.py:39
  49.8 0.0 reduce-scatter.2.cloned.1.call-start
  50.5 0.0 copy-done.4
  50.6 0.0 copy-done.3
  50.6 93.6 %all-to-all-done.1 = bf16[64,128,256]{2,1,0:T(8,128)(2,1)} async-done(((bf16[64,128,256]{2,1,0:T(8,128)(2,1)}), bf16[64,128,256]{2,1,0:T(8,128)(2,1)}, u32[]{:S(2)}, u32[]{:S(2)}) %all-to-all-start.1) | async-done | bytes 4194336 | tf_op jit(solution)/shard_map/all_to_all | solution.py:39
  144.2 4.7 gather_fusion.1
  149.0 0.0 copy-done
  149.0 5.9 multiply_bitcast_fusion.2
  154.9 6.5 copy.38
  161.4 0.1 broadcast.166.clone.1
  161.5 9.4 scatter_fusion
  170.9 27.8 %all-reduce.6 = bf16[1024,256]{1,0:T(8,128)(2,1)S(1)} all-reduce(f32[1024,256]{1,0:T(8,128)S(1)} %bitcast.75), channel_id=1, replica_groups=mesh['rows'=64,'grp'=4] {'grp'}, use_global_device_ids=true, to_apply=%region_1.0 | all-reduce | flops 262144 | bytes 1572864 | tf_op jit(solution)/shard_map/psum | solution.py:13
  198.7 2.6 gather_fusion.2
  201.3 5.9 multiply_bitcast_fusion.1
  207.2 6.6 copy.40
  213.8 4.2 broadcast_in_dim.3
  218.1 14.7 %scatter_fusion.1 = f32[64,128,256]{2,1,0:T(8,128)} fusion(f32[64,128,256]{2,1,0:T(8,128)} %broadcast_in_dim.3, s32[48]{0:T(128)S(1)} %bitcast.83, f32[48,128,256]{2,1,0:T(8,128)} %copy.40), kind=kCustom, calls=%fused_computation.6 | custom fusion | flops 1572864 | bytes 18874560 | tf_op jit(solution)/shard_map/scatter-add | solution.py:44
  232.8 197.8 %all_to_all.27 = f32[64,128,256]{2,1,0:T(8,128)} all-to-all(f32[64,128,256]{2,1,0:T(8,128)} %scatter_fusion.1), channel_id=1, replica_groups=mesh['rows'=64,'grp'=4] {'rows'}, dimensions={0} | all-to-all | bytes 16777216 | tf_op jit(solution)/shard_map/all_to_all | solution.py:45
  430.6 0.1 broadcast.166.clone
  430.7 12.4 %scatter_fusion.2 = f32[8,128,256]{2,1,0:T(8,128)S(1)} fusion(f32[8,128,256]{2,1,0:T(8,128)S(1)} %broadcast.166.clone, s32[64]{0:T(128)S(1)} %reduce.12, f32[64,128,256]{2,1,0:T(8,128)} %all_to_all.27), kind=kCustom, calls=%fused_computation.7 | custom fusion | flops 2097152 | bytes 25166080 | tf_op jit(solution)/shard_map/scatter-add | solution.py:46
  443.1 23.7 %all-reduce.7 = bf16[1024,256]{1,0:T(8,128)(2,1)S(1)} all-reduce(f32[1024,256]{1,0:T(8,128)S(1)} %bitcast.74), channel_id=1, replica_groups=mesh['rows'=64,'grp'=4] {'grp'}, use_global_device_ids=true, to_apply=%region_4.0 | all-reduce | flops 262144 | bytes 1572864 | tf_op jit(solution)/shard_map/psum | solution.py:13
  466.8 2.8 gather_fusion.3
  469.6 108.6 %all_to_all.28 = bf16[64,128,256]{2,1,0:T(8,128)(2,1)} all-to-all(bf16[64,128,256]{2,1,0:T(8,128)(2,1)} %gather_fusion.3), channel_id=1, replica_groups=mesh['rows'=64,'grp'=4] {'rows'}, dimensions={0} | all-to-all | bytes 8388608 | tf_op jit(solution)/shard_map/all_to_all | solution.py:48
  578.2 4.7 gather_fusion.4
  582.9 5.9 multiply_bitcast_fusion
  588.8 6.5 copy.42
  595.4 0.1 broadcast.166
  595.4 9.4 scatter_fusion.3
  604.9 0.0 copy-start.1
  604.9 1.0 copy-done.1
  605.8 0.0 reduce-scatter.2.cloned.1.call-update
  605.9 0.3 all-reduce.5.cloned.1.call-start
  606.1 22.8 %reduce-scatter.2.cloned.1.call-done = f32[256,256]{1,0:T(8,128)} async-done(((f32[1024,256]{1,0:T(8,128)}), f32[256,256]{1,0:T(8,128)}) %reduce-scatter.2.cloned.1.call-update) | async-done | bytes 262160 | tf_op jit(solution)/shard_map/reduce_scatter | solution.py:50
  628.9 2.4 fusion.16
  631.3 0.0 all-reduce.5.cloned.1.call-update
  631.4 254.5 %all-reduce.5.cloned.1.call-done = f32[256,256]{0,1:T(8,128)} async-done(((f32[256,256]{0,1:T(8,128)}), f32[256,256]{0,1:T(8,128)}) %all-reduce.5.cloned.1.call-update) | async-done | bytes 262160 | tf_op jit(solution)/shard_map/psum | solution.py:54
  885.9 1.1 copy.44
  887.0 1.0 fusion.3
  888.0 11.7 %cholesky.50 = f32[128,128]{1,0:T(8,128)S(1)} custom-call(f32[128,128]{1,0:T(8,128)S(1)} %cholesky.118), custom_call_target="Cholesky" | custom-call | tf_op jit(solution)/shard_map/jit(cholesky)/cholesky | solution.py:55
  899.8 9.8 %custom-call.14 = f32[1,128,128]{1,2,0:T(8,128)S(1)} custom-call(f32[1,128,128]{2,1,0:T(8,128)S(1)} %get-tuple-element.33), custom_call_target="InvertDiagBlocksLowerTriangular" | custom-call | tf_op jit(solution)/shard_map/jit(cholesky)/cholesky | solution.py:55
  909.6 0.2 constant_dynamic-update-slice_fusion.1
  909.8 0.3 convolution_subtract_fusion.1
  910.1 11.7 %cholesky.105 = f32[128,128]{1,0:T(8,128)S(1)} custom-call(f32[128,128]{1,0:T(8,128)S(1)} %convolution_subtract_fusion.1), custom_call_target="Cholesky" | custom-call | tf_op jit(solution)/shard_map/jit(cholesky)/cholesky | solution.py:55
  921.8 0.7 compare_reduce_fusion
  923.9 0.1 triangular_solve.58
  924.0 4.3 while.1
  924.2 0.6 fusion.27
  924.8 1.4 bitcast_dynamic-update-slice_fusion.2
  926.3 0.6 fusion.27
  926.9 1.4 bitcast_dynamic-update-slice_fusion.2
  928.3 19.7 %custom-call.15 = f32[2,128,128]{1,2,0:T(8,128)S(1)} custom-call(f32[2,128,128]{2,1,0:T(8,128)S(1)} %get-tuple-element.9), custom_call_target="InvertDiagBlocksLowerTriangular" | custom-call | tf_op jit(solution)/shard_map/triangular_solve | solution.py:58
  948.0 0.0 copy-done.2
  948.0 0.3 fusion.5
  948.3 0.4 convolution_subtract_fusion
  948.7 0.3 fusion.7
  949.1 0.8 copy.45
  949.9 0.8 copy.46
  (20 shorter events, 0.2 us)
Async XLA Ops:
  7.2 141.8 %copy-start = (bf16[1,1,48,128,128]{4,3,2,1,0:T(8,128)(2,1)S(1)}, bf16[1,1,48,128,128]{4,3,2,1,0:T(8,128)(2,1)}, u32[]{:S(2)}) copy-start(bf16[1,1,48,128,128]{4,3,2,1,0:T(8,128)(2,1)} %param.6) | copy-start | bytes 4718596
  8.7 24.4 %all-to-all-start = ((s32[64,1,1]{2,1,0:T(1,128)}), s32[64,1,1]{2,1,0:T(1,128)S(1)}, u32[]{:S(2)}, u32[]{:S(2)}) async-start(s32[64,1,1]{2,1,0:T(1,128)} %copy.36), calls=%async_computation | async-start | bytes 65536 | tf_op jit(solution)/shard_map/all_to_all | solution.py:29
  37.1 13.4 %copy-start.4 = (s32[1,1,48]{2,1,0:T(1,128)S(1)}, s32[1,1,48]{2,1,0:T(1,128)}, u32[]{:S(2)}) copy-start(s32[1,1,48]{2,1,0:T(1,128)} %param.8) | copy-start | bytes 580
  37.1 13.4 %copy-start.3 = (s32[1,1,48]{2,1,0:T(1,128)S(1)}, s32[1,1,48]{2,1,0:T(1,128)}, u32[]{:S(2)}) copy-start(s32[1,1,48]{2,1,0:T(1,128)} %param.7) | copy-start | bytes 580
  37.1 107.1 %all-to-all-start.1 = ((bf16[64,128,256]{2,1,0:T(8,128)(2,1)}), bf16[64,128,256]{2,1,0:T(8,128)(2,1)}, u32[]{:S(2)}, u32[]{:S(2)}) async-start(bf16[64,128,256]{2,1,0:T(8,128)(2,1)} %gather_fusion), calls=%async_computation.1 | async-start | bytes 8388608 | tf_op jit(solution)/shard_map/all_to_all | solution.py:39
  49.8 579.1 %reduce-scatter.2.cloned.1.call-start = ((), (), s32[]{:S(2)}) async-start(), calls=%async_computation.5 | async-start | bytes 1310720 | tf_op jit(solution)/shard_map/reduce_scatter | solution.py:50
  604.9 1.0 copy-start.1
  605.9 280.0 %all-reduce.5.cloned.1.call-start = ((), (), s32[]{:S(2)}) async-start(), calls=%async_computation.6 | async-start | bytes 524288 | tf_op jit(solution)/shard_map/psum | solution.py:54
  628.9 319.1 %copy-start.2 = (f32[256,256]{1,0:T(8,128)S(1)}, f32[256,256]{1,0:T(8,128)}, u32[]{:S(2)}) copy-start(f32[256,256]{1,0:T(8,128)} %reduce-scatter.2.cloned.1.call-done) | copy-start | bytes 786436
Sparse Core Ops, SparseCore 0:
  606.0 22.9 reduce-scatter.1
  635.8 250.0 all-reduce.4
where the time goes:
time: 959 us; the launch traced here: 958 us
  waiting for transfers between devices  371 us (39%)
  blocking collectives  369 us (38%)
  other arithmetic  102 us (11%)
  local copies, waits for them, and re-layouts  51.2 us (5%)
  starting transfers between devices  26.1 us (3%)
  matrix products  21.6 us (2%)
  between operations  16.3 us (2%)
    psum x1, waiting for transfers between devices, per_device(): gram_sum = lax.psum(partial_value, ('rows', 'grp'))  255 us
    all_to_all x1, blocking collectives, per_device(): lax.all_to_all(outgoing, 'rows', split_axis=0, concat_axis=0, tiled=True)  198 us
    all_to_all x1, blocking collectives, per_device(): lax.all_to_all(w_full[requests], 'rows', split_axis=0, concat_axis=0, til...  109 us
    all_to_all x1, waiting for transfers between devices, per_device(): lax.all_to_all(omega_local[requests], 'rows', split_axis=0, concat_axis=0...  93.6 us
    psum x2, blocking collectives, reduce_group(): summed = lax.psum(flattened, 'grp').astype(jnp.bfloat16)  51.4 us
    another operation x6, other arithmetic, per_device(): factor_low = jnp.linalg.cholesky(gram_sum)  34 us
    reduce_scatter x1, waiting for transfers between devices, per_device(): lax.psum_scatter(y_part.reshape(-1, columns), 'grp', scatter_dimension=0,...  22.8 us
    another operation x2, other arithmetic, per_device(): lax.linalg.triangular_solve(factor_low, y_local, left_side=False, lower=T...  19.7 us
  transfers between devices with their start and end apart: 4, of which 3 were waited for; matrix products, arithmetic and copies ran while one was open for 0% of the time, Pallas kernels for 0%

commit v1 on v0

v1 whole, which is shorter than its diff:
```python
import functools
import math

import jax
import jax.numpy as jnp
from jax import lax
from jax.experimental import pallas as pl
from jax.experimental.pallas import tpu as pltpu
from jax.sharding import PartitionSpec as P

RBD = 8
LANES = 128
MESH = pl.DeviceIdType.MESH
SLOT, ROW, PREV_ROW, PREV_SLOT, LAST_ROW, LAST_SLOT = range(6)


def chains(tile_row, tile_slot, tile_count):
    total = tile_row.shape[0]
    order = jnp.arange(total, dtype=jnp.int32)
    live = order < tile_count
    lane = jnp.arange(LANES, dtype=jnp.int32)
    pad = lambda values: jnp.pad(values, (0, LANES - total))
    keys = jnp.stack([tile_row, tile_slot, tile_row, tile_slot])
    query = jnp.stack([pad(tile_row), pad(tile_slot), lane, lane])
    bound = jnp.stack([lane, lane, jnp.full_like(lane, total), jnp.full_like(lane, total)])
    hit = (keys[:, None, :] == query[:, :, None]) & live & (order < bound[:, :, None])
    found = jnp.max(jnp.where(hit, order + 1, 0), axis=2)
    head = jnp.stack([pad(tile_slot), pad(tile_row)])
    return jnp.concatenate([head, found, jnp.zeros((2, LANES), jnp.int32)], axis=0)


def apply_kernel(
    n_rows, n_grp, slots, chunks,
    tiles_ref, omega_ref, meta_ref, want_ref, out_ref,
    tbuf, meta_all, meta_s, want_all, want_s, prev_v, prev_s, last_v, last_s,
    omega_all, ghosts, ghost_out, partial, z_blocks,
    contrib_out, contrib_in, w_partial, w_blocks, w_ghosts, w_ghost_out, y_blocks, y_in,
    local_sem, small_send, small_recv, omega_send, omega_recv, want_send, want_recv,
    right_send, right_recv, left_send, left_recv, fwd_send, fwd_recv,
    ghost_send, ghost_recv, contrib_send, contrib_recv, wg_send, wg_recv, y_send, y_recv,
):
    me = lax.axis_index("rows")
    grp = lax.axis_index("grp")
    per = slots // chunks
    owned = RBD // n_grp
    group = lambda step: lax.rem(grp + step, n_grp)
    peer = lambda step: lax.rem(me + step, n_rows)
    right, left = group(1), group(n_grp - 1)

    barrier = pltpu.get_barrier_semaphore()

    def greet(step, carry):
        pl.semaphore_signal(barrier, inc=1, device_id={"rows": peer(step)}, device_id_type=MESH)
        return carry

    for step in range(1, n_grp):
        pl.semaphore_signal(barrier, inc=1, device_id={"grp": group(step)}, device_id_type=MESH)
    lax.fori_loop(1, n_rows, greet, 0)
    pl.semaphore_wait(barrier, n_rows - 1 + n_grp - 1)

    def over_x(src, dst, send, recv, to):
        return pltpu.make_async_remote_copy(
            src_ref=src, dst_ref=dst, send_sem=send, recv_sem=recv, device_id={"grp": to}, device_id_type=MESH)

    def over_rows(src, dst, send, recv, to):
        return pltpu.make_async_remote_copy(
            src_ref=src, dst_ref=dst, send_sem=send, recv_sem=recv, device_id={"rows": to}, device_id_type=MESH)

    def want_copy(step):
        return over_rows(want_ref, want_all.at[me], want_send.at[step], want_recv.at[step], peer(step))

    def want_arrival(step):
        came = lax.rem(me - step + n_rows, n_rows)
        return over_rows(want_ref, want_all.at[came], want_send.at[step], want_recv.at[step], peer(step))

    def meta_copy(step):
        place = (0, 1, 3, 2)[step]
        return over_x(meta_ref, meta_all.at[place], small_send.at[step], small_recv.at[step], group(step))

    def omega_copy(step):
        to = group(step)
        return over_x(
            omega_ref.at[to], omega_all.at[pl.ds(grp * owned, owned)], omega_send.at[step], omega_recv.at[step], to)

    def omega_arrival(step):
        came = group(n_grp - step)
        return over_x(
            omega_ref.at[came], omega_all.at[pl.ds(came * owned, owned)], omega_send.at[step], omega_recv.at[step], came)

    def start_want(step, carry):
        want_copy(step).start()
        return carry

    lax.fori_loop(1, n_rows, start_want, 0)
    for step in range(1, n_grp):
        omega_copy(step).start()
        meta_copy(step).start()

    own_tiles = pltpu.make_async_copy(tiles_ref, tbuf.at[0], local_sem.at[0])
    own_tiles.start()

    def to_right(c):
        part = pl.ds(c * per, per)
        return over_x(tiles_ref.at[part], tbuf.at[1, part], right_send.at[c], right_recv.at[c], right)

    def to_left(c):
        part = pl.ds(c * per, per)
        return over_x(tiles_ref.at[part], tbuf.at[2, part], left_send.at[c], left_recv.at[c], left)

    def forward(c):
        part = pl.ds(c * per, per)
        if c < chunks // 2:
            return over_x(tbuf.at[1, part], tbuf.at[3, part], fwd_send.at[c], fwd_recv.at[c], right)
        return over_x(tbuf.at[2, part], tbuf.at[3, part], fwd_send.at[c], fwd_recv.at[c], left)

    for c in range(chunks):
        to_right(c).start()
        to_left(c).start()

    want_all[me] = want_ref[...]
    for j in range(owned):
        omega_all[grp * owned + j] = omega_ref[grp, j]
    meta_all[0] = meta_ref[...]
    partial[:, 0] = jnp.zeros((n_grp,) + partial.shape[2:], jnp.float32)
    w_partial[0] = jnp.zeros(w_partial.shape[1:], jnp.float32)

    def wait_want(step, carry):
        want_arrival(step).wait_recv()
        return carry

    lax.fori_loop(1, n_rows, wait_want, 0)
    want_down = pltpu.make_async_copy(want_all, want_s, local_sem.at[1])
    want_down.start()
    for step in range(1, n_grp):
        meta_copy(step).wait_recv()
        omega_arrival(step).wait_recv()
    meta_down = pltpu.make_async_copy(meta_all, meta_s, local_sem.at[2])
    meta_down.start()
    want_down.wait()
    meta_down.wait()

    def ghost_copy(step):
        return over_rows(ghost_out.at[step], ghosts.at[step], ghost_send.at[step], ghost_recv.at[step], peer(step))

    def start_ghost(step, carry):
        ghost_out[step] = omega_all[want_s[peer(step), 0, me]]
        ghost_copy(step).start()
        return carry

    ghosts[0] = omega_all[want_s[me, 0, me]]
    lax.fori_loop(1, n_rows, start_ghost, 0)

    blocks = lax.broadcasted_iota(jnp.int32, (RBD, LANES), 0)

    def link(step, last):
        row = want_all[lax.rem(me - step + n_rows, n_rows)]
        hit = blocks == row
        prev_v[step] = jnp.max(jnp.where(hit, last, 0), axis=0, keepdims=True)
        return jnp.where(hit, step + 1, last)

    last_v[...] = lax.fori_loop(0, n_rows, link, jnp.zeros((RBD, LANES), jnp.int32))
    prev_down = pltpu.make_async_copy(prev_v, prev_s, local_sem.at[1])
    last_down = pltpu.make_async_copy(last_v, last_s, local_sem.at[2])
    prev_down.start()
    last_down.start()
    prev_down.wait()
    last_down.wait()

    own_tiles.wait()
    for c in range(chunks):
        to_right(c).wait_recv()
        if c < chunks // 2:
            forward(c).start()
        to_left(c).wait_recv()
        if c >= chunks // 2:
            forward(c).start()

    def wait_ghost(step, carry):
        ghost_copy(step).wait_recv()
        return carry

    lax.fori_loop(1, n_rows, wait_ghost, 0)

    unroll = per

    def multiply(place, first, source, by_row, sent):
        prev_key = PREV_ROW if by_row else PREV_SLOT
        products = []
        for i in range(unroll):
            t = first + i
            tile = tbuf[place, t]
            if by_row:
                slot = meta_s[place, SLOT, t]
                block = source[lax.rem(me - slot + n_rows, n_rows)]
                product = lax.dot_general(block, tile, (((1,), (1,)), ((), ())), preferred_element_type=jnp.float32)
            else:
                block = source[meta_s[place, ROW, t]]
                product = lax.dot_general(block, tile, (((1,), (0,)), ((), ())), preferred_element_type=jnp.float32)
            products.append(product)
        for i in range(unroll):
            t = first + i
            partial[place, t + 1] = products[i] + partial[place, meta_s[place, prev_key, t]]

    def whole(place, source, by_row):
        def step(c, carry):
            multiply(place, c * unroll, source, by_row, None)
            return carry
        lax.fori_loop(0, slots // unroll, step, 0)

    def total(key, index):
        value = partial[0, meta_s[0, key, index]]
        for place in range(1, n_grp):
            value = value + partial[place, meta_s[place, key, index]]
        return value

    for place in range(3):
        whole(place, ghosts, True)
    for c in range(chunks):
        forward(c).wait_recv()
        multiply(3, c * per, ghosts, True, None)

    def close_z(b, carry):
        z_blocks[b] = total(LAST_ROW, b).astype(jnp.bfloat16)
        return carry

    lax.fori_loop(0, RBD, close_z, 0)

    for place in range(n_grp):
        whole(place, z_blocks, False)

    def contrib_copy(step):
        return over_rows(
            contrib_out.at[step], contrib_in.at[step], contrib_send.at[step], contrib_recv.at[step], peer(step))

    contrib_in[0] = total(LAST_SLOT, me).astype(jnp.bfloat16)

    def start_contrib(step, carry):
        contrib_out[step] = total(LAST_SLOT, peer(step)).astype(jnp.bfloat16)
        contrib_copy(step).start()
        return carry

    lax.fori_loop(1, n_rows, start_contrib, 0)

    def add_contrib(step):
        w_partial[step + 1] = contrib_in[step].astype(jnp.float32) + w_partial[prev_s[step, 0, me]]

    add_contrib(0)

    def take_contrib(step, carry):
        contrib_copy(step).wait_recv()
        add_contrib(step)
        return carry

    lax.fori_loop(1, n_rows, take_contrib, 0)

    def close_w(b, carry):
        w_blocks[b] = w_partial[last_s[b, me]].astype(jnp.bfloat16)
        return carry

    lax.fori_loop(0, RBD, close_w, 0)

    def wg_copy(step):
        return over_rows(w_ghost_out.at[step], w_ghosts.at[step], wg_send.at[step], wg_recv.at[step], peer(step))

    def start_wg(step, carry):
        w_ghost_out[step] = w_blocks[want_s[peer(step), 0, me]]
        wg_copy(step).start()
        return carry

    def wait_wg(step, carry):
        wg_copy(step).wait_recv()
        return carry

    w_ghosts[0] = w_blocks[want_s[me, 0, me]]
    lax.fori_loop(1, n_rows, start_wg, 0)
    lax.fori_loop(1, n_rows, wait_wg, 0)

    for place in range(n_grp):
        whole(place, w_ghosts, True)

    def close_y(b, carry):
        y_blocks[b] = total(LAST_ROW, b)
        return carry

    lax.fori_loop(0, RBD, close_y, 0)

    def y_copy(step):
        to = group(step)
        return over_x(
            y_blocks.at[pl.ds(to * owned, owned)], y_in.at[step], y_send.at[step], y_recv.at[step], to)

    for step in range(1, n_grp):
        y_copy(step).start()
    for j in range(owned):
        y_in[0, j] = y_blocks[grp * owned + j]
    for step in range(1, n_grp):
        y_copy(step).wait_recv()
    width = out_ref.shape[0] // n_grp
    for step in range(n_grp):
        came = group(n_grp - step) if step else grp
        for j in range(owned):
            out_ref[pl.ds(pl.multiple_of(came * width, width), width), pl.ds(j * LANES, LANES)] = y_in[step, j]

    def drain(step, carry):
        want_copy(step).wait_send()
        ghost_copy(step).wait_send()
        contrib_copy(step).wait_send()
        wg_copy(step).wait_send()
        return carry

    lax.fori_loop(1, n_rows, drain, 0)
    for step in range(1, n_grp):
        meta_copy(step).wait_send()
        omega_copy(step).wait_send()
        y_copy(step).wait_send()
    for c in range(chunks):
        to_right(c).wait_send()
        to_left(c).wait_send()
        forward(c).wait_send()


def apply_all(tiles, omega_parts, meta, want_row, n_rows, n_grp, chunks):
    slots, tile, _ = tiles.shape
    owned = RBD // n_grp
    width = omega_parts.shape[2]
    block = (width, tile)
    bf16, f32, i32 = jnp.bfloat16, jnp.float32, jnp.int32
    dma = lambda count: pltpu.SemaphoreType.DMA((count,))
    vmem = pl.BlockSpec(memory_space=pltpu.VMEM)
    scratch = [
        pltpu.VMEM((n_grp, slots, tile, tile), bf16),
        pltpu.VMEM((n_grp, 8, LANES), i32),
        pltpu.SMEM((n_grp, 8, LANES), i32),
        pltpu.VMEM((n_rows, 1, LANES), i32),
        pltpu.SMEM((n_rows, 1, LANES), i32),
        pltpu.VMEM((n_rows, 1, LANES), i32),
        pltpu.SMEM((n_rows, 1, LANES), i32),
        pltpu.VMEM((RBD, LANES), i32),
        pltpu.SMEM((RBD, LANES), i32),
        pltpu.VMEM((RBD,) + block, bf16),
        pltpu.VMEM((n_rows,) + block, bf16),
        pltpu.VMEM((n_rows,) + block, bf16),
        pltpu.VMEM((n_grp, slots + 1) + block, f32),
        pltpu.VMEM((RBD,) + block, bf16),
        pltpu.VMEM((n_rows,) + block, bf16),
        pltpu.VMEM((n_rows,) + block, bf16),
        pltpu.VMEM((n_rows + 1,) + block, f32),
        pltpu.VMEM((RBD,) + block, bf16),
        pltpu.VMEM((n_rows,) + block, bf16),
        pltpu.VMEM((n_rows,) + block, bf16),
        pltpu.VMEM((RBD,) + block, f32),
        pltpu.VMEM((n_grp, owned) + block, f32),
        dma(3), dma(n_grp), dma(n_grp), dma(n_grp), dma(n_grp), dma(n_rows), dma(n_rows),
        dma(chunks), dma(chunks), dma(chunks), dma(chunks), dma(chunks), dma(chunks),
        dma(n_rows), dma(n_rows), dma(n_rows), dma(n_rows), dma(n_rows), dma(n_rows), dma(n_grp), dma(n_grp),
    ]
    return pl.pallas_call(
        functools.partial(apply_kernel, n_rows, n_grp, slots, chunks),
        out_shape=jax.ShapeDtypeStruct((width * n_grp, owned * tile), f32),
        in_specs=[pl.BlockSpec(memory_space=pl.ANY), vmem, vmem, vmem],
        out_specs=vmem,
        scratch_shapes=scratch,
        compiler_params=pltpu.CompilerParams(
            collective_id=0, has_side_effects=True, vmem_limit_bytes=40 * 1024 * 1024),
        name="apply_all",
    )(tiles, omega_parts, meta, want_row)


def per_device(tiles, tile_row, tile_slot, tile_count, want, omega):
    tile = tiles.shape[-1]
    slots = tiles.shape[2]
    columns = omega.shape[1]
    n_rows = lax.axis_size("rows")
    n_grp = lax.axis_size("grp")
    highest = lax.Precision.HIGHEST
    chunks = 8 if slots % 8 == 0 and slots >= 48 else 2
    owned = RBD // n_grp
    meta = chains(tile_row.reshape(slots), tile_slot.reshape(slots), tile_count.reshape(()))
    want_row = jnp.pad(want.reshape(1, n_rows), ((0, 0), (0, LANES - n_rows)))
    omega_parts = omega.reshape(owned, tile, n_grp, columns // n_grp).transpose(2, 0, 3, 1)
    y_t = apply_all(tiles.reshape(slots, tile, tile), omega_parts, meta, want_row, n_rows, n_grp, chunks)
    partial_gram = lax.dot_general(
        y_t, y_t, (((1,), (1,)), ((), ())), precision=highest, preferred_element_type=jnp.float32)
    gram = lax.psum(lax.psum(partial_gram, "grp"), "rows")
    factor_low = jnp.linalg.cholesky(gram)
    norm_scale = math.sqrt(n_rows * RBD * tile)
    basis = (
        lax.linalg.triangular_solve(factor_low, y_t.T, left_side=False, lower=True, transpose_a=True) * norm_scale
    )
    return (basis, factor_low.T / norm_scale)


def solution(mesh):
    return jax.shard_map(
        per_device,
        mesh=mesh,
        in_specs=(
            P("rows", "grp", None, None, None),
            P("rows", "grp", None),
            P("rows", "grp", None),
            P("rows", "grp"),
            P("rows", None),
            P(("rows", "grp"), None),
        ),
        out_specs=(P(("rows", "grp"), None), P()),
        check_vma=False,
    )
```

time: 959 us -> 456 us (0.48)
  blocking collectives: 369 us -> 0 us
  waiting for transfers between devices: 371 us -> 225 us
  Pallas kernels: 0 us -> 144 us
  other arithmetic: 102 us -> 56.4 us
  local copies, waits for them, and re-layouts: 51.2 us -> 11.1 us
  starting transfers between devices: 26.1 us -> 0.26 us
  matrix products: 21.6 us -> 2.49 us
    all_to_all x2 -> x0, blocking collectives: 306 us -> none  [the longest x1 198 us: per_device(): lax.all_to_all(outgoing, 'rows', split_axis=0, concat_axis=0, tiled=True)]
    pallas_call x0 -> x1, Pallas kernels: none -> 144 us  [apply_all(): pl.pallas_call(functools.partial(apply_kernel, n_rows, n_grp, slots, chun...]
    all_to_all x2 -> x0, waiting for transfers between devices: 93.6 us -> none  [the longest x1 93.6 us: per_device(): lax.all_to_all(omega_local[requests], 'rows', split_axis=0, concat_axis=0...]
    psum x2 -> x0, blocking collectives: 51.4 us -> none  [reduce_group(): summed = lax.psum(flattened, 'grp').astype(jnp.bfloat16)]
    scatter-add x4 -> x0, other arithmetic: 45.9 us -> none  [the longest x2 18.8 us: forward(): return jax.ops.segment_sum(product * live_weight, row_ids, num_segments=RBD)]
    psum x1 -> x2, waiting for transfers between devices: 255 us -> 225 us  [per_device(): gram = lax.psum(lax.psum(partial_gram, 'grp'), 'rows')]
    all_to_all x2 -> x0, starting transfers between devices: 25.8 us -> none  [the longest x1 13.2 us: per_device(): lax.all_to_all(want.reshape(owners, 1), 'rows', split_axis=0, concat_axis...]
    reduce_scatter x1 -> x0, waiting for transfers between devices: 22.8 us -> none  [per_device(): lax.psum_scatter(y_part.reshape(-1, columns), 'grp', scatter_dimension=0,...]
  transfers between devices with their start and end apart: 4 -> 2, of which waited for: 3 -> 2; matrix products, arithmetic and copies ran while one was open for 0% -> 0% of each run, Pallas kernels for 0% -> 0%
where the time goes in v1:
time: 456 us
  waiting for transfers between devices  225 us (49%)
  Pallas kernels  144 us (32%)
  other arithmetic  56.4 us (12%)
  between operations  16.2 us (4%)
  local copies, waits for them, and re-layouts  11.1 us (2%)
    psum x2, waiting for transfers between devices, per_device(): gram = lax.psum(lax.psum(partial_gram, 'grp'), 'rows')  225 us
    pallas_call x1, Pallas kernels, apply_all(): pl.pallas_call(functools.partial(apply_kernel, n_rows, n_grp, slots, chun...  144 us
    another operation x7, other arithmetic, per_device(): factor_low = jnp.linalg.cholesky(gram)  34.7 us
    another operation x2, other arithmetic, per_device(): lax.linalg.triangular_solve(factor_low, y_t.T, left_side=False, lower=Tru...  19.7 us
  transfers between devices with their start and end apart: 2, of which 2 were waited for; matrix products, arithmetic and copies ran while one was open for 0% of the time, Pallas kernels for 0%

profile of v1, /device:TPU:1, one launch (start us, length us, event | category | flops | bytes accessed | tf_op | source)
XLA Modules:
  0.0 455.8 jit_solution(10890636014381886070)
XLA Ops:
  7.2 0.0 all-reduce.7.cloned.1.call-start
  7.9 0.1 pad.27.clone
  8.0 0.1 pad.24.clone
  8.0 0.7 pad.16.want_ref
  8.7 1.1 reshape.67
  9.8 0.2 copy.19
  10.0 0.7 pad_bitcast_fusion
  10.6 0.1 add_add_fusion.1
  10.7 0.7 pad_add_fusion
  11.5 0.1 select_reduce_fusion
  11.6 0.1 add_add_fusion.meta_ref
  11.7 0.0 copy-start
  11.7 1.4 copy-done
  13.1 143.7 %apply_all.1 = f32[256,256]{1,0:T(8,128)S(1)} custom-call(bf16[48,128,128]{2,1,0:T(8,128)(2,1)S(1)} %bitcast.50, bf16[4,2,64,128]{3,2,1,0:T(8,128)(2,1)S(1)} %bitcast.51, s32[8,128]{1,0:T(8,128)S(1)} %add_add_fusion.meta_ref, s32[1,128]{1,0:T(1,128)S(1)} %pad.16.want_ref), custom_call_target="tpu_custom_call" | custom-call | tf_op jit(solution)/shard_map/apply_all/pallas_call | solution.py:357
  156.8 1.1 fusion.11
  157.9 0.0 all-reduce.7.cloned.1.call-update
  157.9 0.2 all-reduce.9.cloned.1.call-start
  158.2 43.6 %all-reduce.7.cloned.1.call-done = f32[256,256]{0,1:T(8,128)} async-done(((f32[256,256]{0,1:T(8,128)}), f32[256,256]{0,1:T(8,128)}) %all-reduce.7.cloned.1.call-update) | async-done | bytes 262160 | tf_op jit(solution)/shard_map/psum | solution.py:384
  201.8 0.0 all-reduce.9.cloned.1.call-update
  201.8 181.8 %all-reduce.9.cloned.1.call-done = f32[256,256]{0,1:T(8,128)} async-done(((f32[256,256]{0,1:T(8,128)}), f32[256,256]{0,1:T(8,128)}) %all-reduce.9.cloned.1.call-update) | async-done | bytes 262160 | tf_op jit(solution)/shard_map/psum | solution.py:384
  383.6 1.1 copy.21
  384.7 1.0 fusion
  385.7 11.7 %cholesky.50 = f32[128,128]{1,0:T(8,128)S(1)} custom-call(f32[128,128]{1,0:T(8,128)S(1)} %cholesky.118), custom_call_target="Cholesky" | custom-call | tf_op jit(solution)/shard_map/jit(cholesky)/cholesky | solution.py:385
  397.5 9.8 %custom-call.14 = f32[1,128,128]{1,2,0:T(8,128)S(1)} custom-call(f32[1,128,128]{2,1,0:T(8,128)S(1)} %get-tuple-element.31), custom_call_target="InvertDiagBlocksLowerTriangular" | custom-call | tf_op jit(solution)/shard_map/jit(cholesky)/cholesky | solution.py:385
  407.3 0.2 constant_dynamic-update-slice_fusion.1
  407.5 0.3 convolution_subtract_fusion.1
  407.8 11.7 %cholesky.105 = f32[128,128]{1,0:T(8,128)S(1)} custom-call(f32[128,128]{1,0:T(8,128)S(1)} %convolution_subtract_fusion.1), custom_call_target="Cholesky" | custom-call | tf_op jit(solution)/shard_map/jit(cholesky)/cholesky | solution.py:385
  419.6 0.7 compare_reduce_fusion
  420.3 0.6 compare_reduce_fusion.1
  422.3 0.1 triangular_solve.58
  422.4 4.3 while.1
  422.6 0.6 fusion.19
  423.1 1.4 bitcast_dynamic-update-slice_fusion.2
  424.6 0.6 fusion.19
  425.2 1.4 bitcast_dynamic-update-slice_fusion.2
  426.6 19.7 %custom-call.15 = f32[2,128,128]{1,2,0:T(8,128)S(1)} custom-call(f32[2,128,128]{2,1,0:T(8,128)S(1)} %get-tuple-element.9), custom_call_target="InvertDiagBlocksLowerTriangular" | custom-call | tf_op jit(solution)/shard_map/triangular_solve | solution.py:388
  446.3 0.3 fusion.2
  446.6 0.3 convolution_subtract_fusion
  446.9 0.3 fusion.5
  447.3 0.8 copy.23
  448.1 0.8 copy.24
  (17 shorter events, 0.2 us)
Async XLA Ops:
  7.2 194.6 %all-reduce.7.cloned.1.call-start = ((), (), s32[]{:S(2)}) async-start(), calls=%async_computation | async-start | bytes 524288 | tf_op jit(solution)/shard_map/psum | solution.py:384
  11.7 1.4 copy-start
  157.9 225.7 %all-reduce.9.cloned.1.call-start = ((), (), s32[]{:S(2)}) async-start(), calls=%async_computation.1 | async-start | bytes 524288 | tf_op jit(solution)/shard_map/psum | solution.py:384
Sparse Core Ops, SparseCore 0:
  158.0 43.7 all-reduce.6
  205.7 177.9 all-reduce.8

commit v2 on v1

--- a/solution.py
+++ b/solution.py
@@ -31,13 +31,15 @@
 
 def apply_kernel(
     n_rows, n_grp, slots, chunks,
-    tiles_ref, omega_ref, meta_ref, want_ref, out_ref,
+    tiles_ref, omega_ref, meta_ref, want_ref, basis_ref, factor_ref,
     tbuf, meta_all, meta_s, want_all, want_s, prev_v, prev_s, last_v, last_s,
     omega_all, ghosts, ghost_out, partial, z_blocks,
     contrib_out, contrib_in, w_partial, w_blocks, w_ghosts, w_ghost_out, y_blocks, y_in,
+    y_all, gram_out, gram_in, part_out, part_in, row_out, row_in, slice_all, gram_all, work,
     local_sem, small_send, small_recv, omega_send, omega_recv, want_send, want_recv,
     right_send, right_recv, left_send, left_recv, fwd_send, fwd_recv,
     ghost_send, ghost_recv, contrib_send, contrib_recv, wg_send, wg_recv, y_send, y_recv,
+    gram_send, gram_recv, part_send, part_recv, row_send, row_recv, back_send, back_recv, all_send, all_recv,
 ):
     me = lax.axis_index("rows")
     grp = lax.axis_index("grp")
@@ -295,11 +297,122 @@
         y_in[0, j] = y_blocks[grp * owned + j]
     for step in range(1, n_grp):
         y_copy(step).wait_recv()
-    width = out_ref.shape[0] // n_grp
+    width = y_all.shape[0] // n_grp
     for step in range(n_grp):
-        came = group(n_grp - step) if step else grp
+        came = group(n_grp - step)
         for j in range(owned):
-            out_ref[pl.ds(pl.multiple_of(came * width, width), width), pl.ds(j * LANES, LANES)] = y_in[step, j]
+            y_all[pl.ds(pl.multiple_of(came * width, width), width), pl.ds(j * LANES, LANES)] = y_in[step, j]
+
+    inner = part_in.shape[0]
+    outer = n_rows // inner
+    some = part_in.shape[1]
+    spot = lax.rem(me, inner)
+    level = lax.div(me, inner)
+    y_value = y_all[...]
+    own_gram = lax.dot_general(
+        y_value, y_value, (((1,), (1,)), ((), ())), precision=lax.Precision.HIGHEST, preferred_element_type=jnp.float32)
+    gram_out[...] = own_gram.reshape(gram_out.shape)
+
+    def gram_copy(step):
+        to = group(step)
+        return over_x(gram_out.at[to], gram_in.at[grp], gram_send.at[step], gram_recv.at[step], to)
+
+    def gram_arrival(step):
+        came = group(n_grp - step)
+        return over_x(gram_out.at[came], gram_in.at[came], gram_send.at[step], gram_recv.at[step], came)
+
+    for step in range(1, n_grp):
+        gram_copy(step).start()
+    gram_in[grp] = gram_out[grp]
+    for step in range(1, n_grp):
+        gram_arrival(step).wait_recv()
+    summed = gram_in[0]
+    for step in range(1, n_grp):
+        summed = summed + gram_in[step]
+    part_out[...] = summed.reshape(part_out.shape)
+
+    def beside(step):
+        return lax.rem(spot + step, inner)
+
+    def part_copy(step):
+        to = beside(step)
+        return over_rows(
+            part_out.at[to], part_in.at[spot], part_send.at[step], part_recv.at[step], level * inner + to)
+
+    def part_arrival(step):
+        came = beside(inner - step)
+        return over_rows(
+            part_out.at[came], part_in.at[came], part_send.at[step], part_recv.at[step], level * inner + came)
+
+    for step in range(1, inner):
+        part_copy(step).start()
+    part_in[spot] = part_out[spot]
+    for step in range(1, inner):
+        part_arrival(step).wait_recv()
+    summed = part_in[0]
+    for step in range(1, inner):
+        summed = summed + part_in[step]
+    row_out[...] = summed
+
+    def across(step):
+        return lax.rem(level + step, outer)
+
+    def row_copy(step):
+        return over_rows(
+            row_out, row_in.at[level], row_send.at[step], row_recv.at[step], across(step) * inner + spot)
+
+    def row_arrival(step):
+        came = across(outer - step)
+        return over_rows(row_out, row_in.at[came], row_send.at[step], row_recv.at[step], came * inner + spot)
+
+    for step in range(1, outer):
+        row_copy(step).start()
+    row_in[level] = row_out[...]
+    for step in range(1, outer):
+        row_arrival(step).wait_recv()
+    summed = row_in[0]
+    for step in range(1, outer):
+        summed = summed + row_in[step]
+    slice_all[spot] = summed
+
+    def back_copy(step):
+        return over_rows(
+            slice_all.at[spot], slice_all.at[spot], back_send.at[step], back_recv.at[step],
+            level * inner + beside(step))
+
+    def back_arrival(step):
+        came = beside(inner - step)
+        return over_rows(
+            slice_all.at[came], slice_all.at[came], back_send.at[step], back_recv.at[step], level * inner + came)
+
+    for step in range(1, inner):
+        back_copy(step).start()
+    for step in range(1, inner):
+        back_arrival(step).wait_recv()
+    gram_all[grp] = slice_all[...].reshape(gram_all.shape[1:])
+
+    def all_copy(step):
+        return over_x(
+            gram_all.at[grp], gram_all.at[grp], all_send.at[step], all_recv.at[step], group(step))
+
+    def all_arrival(step):
+        came = group(n_grp - step)
+        return over_x(gram_all.at[came], gram_all.at[came], all_send.at[step], all_recv.at[step], came)
+
+    for step in range(1, n_grp):
+        all_copy(step).start()
+    for step in range(1, n_grp):
+        all_arrival(step).wait_recv()
+
+    scale = math.sqrt(n_rows * RBD * LANES)
+    order = work.shape[0]
+    eliminate(gram_all[...].reshape(order, order), work)
+    place_row = lax.broadcasted_iota(jnp.int32, (order, order), 0)
+    place_col = lax.broadcasted_iota(jnp.int32, (order, order), 1)
+    factor_ref[...] = jnp.where(place_col >= place_row, work[:, :order], 0.0) * (1.0 / scale)
+    solved = jnp.dot(
+        work[:, order:], y_value, precision=lax.Precision.HIGHEST, preferred_element_type=jnp.float32)
+    basis_ref[...] = solved.T * scale
 
     def drain(step, carry):
         want_copy(step).wait_send()
@@ -313,10 +426,50 @@
         meta_copy(step).wait_send()
         omega_copy(step).wait_send()
         y_copy(step).wait_send()
+        gram_copy(step).wait_send()
+        all_copy(step).wait_send()
+    for step in range(1, inner):
+        part_copy(step).wait_send()
+        back_copy(step).wait_send()
+    for step in range(1, outer):
+        row_copy(step).wait_send()
     for c in range(chunks):
         to_right(c).wait_send()
         to_left(c).wait_send()
         forward(c).wait_send()
+
+
+BLOCK = 32
+
+
+def eliminate(gram, work):
+    order = gram.shape[0]
+    work[:, :order] = gram
+    place_row = lax.broadcasted_iota(jnp.int32, (order, order), 0)
+    place_col = lax.broadcasted_iota(jnp.int32, (order, order), 1)
+    work[:, order:] = jnp.where(place_row == place_col, 1.0, 0.0)
+    small_row = lax.broadcasted_iota(jnp.int32, (BLOCK, BLOCK), 0)
+    small_col = lax.broadcasted_iota(jnp.int32, (BLOCK, BLOCK), 1)
+    for first in range(0, order, BLOCK):
+        after = first + BLOCK
+        low = first // LANES * LANES
+        high = order + low + LANES
+        left = work[first:after, first:after]
+        right = jnp.where(small_row == small_col, 1.0, 0.0)
+        for k in range(BLOCK):
+            unit = lax.rsqrt(left[k:k + 1, k:k + 1])
+            rows_left = left[k:k + 1, :] * unit
+            rows_right = right[k:k + 1, :] * unit
+            column = jnp.where(small_row[:, :1] > k, left[:, k:k + 1] * unit, 0.0)
+            left = jnp.where(small_row == k, rows_left, left - column * rows_left)
+            right = jnp.where(small_row == k, rows_right, right - column * rows_right)
+        done = jnp.dot(
+            right, work[first:after, low:high], precision=lax.Precision.HIGHEST, preferred_element_type=jnp.float32)
+        work[first:after, low:high] = done
+        if after < order:
+            work[after:, low:high] = work[after:, low:high] - lax.dot_general(
+                done[:, after - low:order - low], done, (((0,), (0,)), ((), ())),
+                precision=lax.Precision.HIGHEST, preferred_element_type=jnp.float32)
 
 
 def apply_all(tiles, omega_parts, meta, want_row, n_rows, n_grp, chunks):
@@ -324,6 +477,9 @@
     owned = RBD // n_grp
     width = omega_parts.shape[2]
     block = (width, tile)
+    order = width * n_grp
+    inner = 8 if n_rows % 8 == 0 else n_rows
+    some = width // inner
     bf16, f32, i32 = jnp.bfloat16, jnp.float32, jnp.int32
     dma = lambda count: pltpu.SemaphoreType.DMA((count,))
     vmem = pl.BlockSpec(memory_space=pltpu.VMEM)
@@ -350,15 +506,30 @@
         pltpu.VMEM((n_rows,) + block, bf16),
         pltpu.VMEM((RBD,) + block, f32),
         pltpu.VMEM((n_grp, owned) + block, f32),
+        pltpu.VMEM((order, owned * tile), f32),
+        pltpu.VMEM((n_grp, width, order), f32),
+        pltpu.VMEM((n_grp, width, order), f32),
+        pltpu.VMEM((inner, some, order), f32),
+        pltpu.VMEM((inner, some, order), f32),
+        pltpu.VMEM((some, order), f32),
+        pltpu.VMEM((n_rows // inner, some, order), f32),
+        pltpu.VMEM((inner, some, order), f32),
+        pltpu.VMEM((n_grp, width, order), f32),
+        pltpu.VMEM((order, 2 * order), f32),
         dma(3), dma(n_grp), dma(n_grp), dma(n_grp), dma(n_grp), dma(n_rows), dma(n_rows),
         dma(chunks), dma(chunks), dma(chunks), dma(chunks), dma(chunks), dma(chunks),
         dma(n_rows), dma(n_rows), dma(n_rows), dma(n_rows), dma(n_rows), dma(n_rows), dma(n_grp), dma(n_grp),
+        dma(n_grp), dma(n_grp), dma(inner), dma(inner), dma(n_rows // inner), dma(n_rows // inner),
+        dma(inner), dma(inner), dma(n_grp), dma(n_grp),
     ]
     return pl.pallas_call(
         functools.partial(apply_kernel, n_rows, n_grp, slots, chunks),
-        out_shape=jax.ShapeDtypeStruct((width * n_grp, owned * tile), f32),
+        out_shape=(
+            jax.ShapeDtypeStruct((owned * tile, order), f32),
+            jax.ShapeDtypeStruct((order, order), f32),
+        ),
         in_specs=[pl.BlockSpec(memory_space=pl.ANY), vmem, vmem, vmem],
-        out_specs=vmem,
+        out_specs=(vmem, vmem),
         scratch_shapes=scratch,
         compiler_params=pltpu.CompilerParams(
             collective_id=0, has_side_effects=True, vmem_limit_bytes=40 * 1024 * 1024),
@@ -372,22 +543,12 @@
     columns = omega.shape[1]
     n_rows = lax.axis_size("rows")
     n_grp = lax.axis_size("grp")
-    highest = lax.Precision.HIGHEST
     chunks = 8 if slots % 8 == 0 and slots >= 48 else 2
     owned = RBD // n_grp
     meta = chains(tile_row.reshape(slots), tile_slot.reshape(slots), tile_count.reshape(()))
     want_row = jnp.pad(want.reshape(1, n_rows), ((0, 0), (0, LANES - n_rows)))
     omega_parts = omega.reshape(owned, tile, n_grp, columns // n_grp).transpose(2, 0, 3, 1)
-    y_t = apply_all(tiles.reshape(slots, tile, tile), omega_parts, meta, want_row, n_rows, n_grp, chunks)
-    partial_gram = lax.dot_general(
-        y_t, y_t, (((1,), (1,)), ((), ())), precision=highest, preferred_element_type=jnp.float32)
-    gram = lax.psum(lax.psum(partial_gram, "grp"), "rows")
-    factor_low = jnp.linalg.cholesky(gram)
-    norm_scale = math.sqrt(n_rows * RBD * tile)
-    basis = (
-        lax.linalg.triangular_solve(factor_low, y_t.T, left_side=False, lower=True, transpose_a=True) * norm_scale
-    )
-    return (basis, factor_low.T / norm_scale)
+    return apply_all(tiles.reshape(slots, tile, tile), omega_parts, meta, want_row, n_rows, n_grp, chunks)
 
 
 def solution(mesh):

time: 456 us -> 202 us (0.44)
  waiting for transfers between devices: 225 us -> 0 us
  other arithmetic: 56.4 us -> 1.03 us
  Pallas kernels: 144 us -> 194 us
  between operations: 16.2 us -> 1.32 us
  local copies, waits for them, and re-layouts: 11.1 us -> 5.56 us
    psum x2 -> x0, waiting for transfers between devices: 225 us -> none  [per_device(): gram = lax.psum(lax.psum(partial_gram, 'grp'), 'rows')]
    another operation x9 -> x0, other arithmetic: 54.3 us -> none  [the longest x7 34.7 us: per_device(): factor_low = jnp.linalg.cholesky(gram)]
    pallas_call x1, Pallas kernels: 144 us -> 194 us  [apply_all(): pl.pallas_call(functools.partial(apply_kernel, n_rows, n_grp, slots, chun...]
  transfers between devices with their start and end apart: 2 -> 0, of which waited for: 2 -> 0; matrix products, arithmetic and copies ran while one was open for 0% -> 0% of each run, Pallas kernels for 0% -> 0%
where the time goes in v2:
time: 202 us
  Pallas kernels  194 us (96%)
  local copies, waits for them, and re-layouts  5.56 us (3%)
    pallas_call x1, Pallas kernels, apply_all(): pl.pallas_call(functools.partial(apply_kernel, n_rows, n_grp, slots, chun...  194 us

profile of v2, /device:TPU:1, one launch (start us, length us, event | category | flops | bytes accessed | tf_op | source)
XLA Modules:
  0.0 202.2 jit_solution(15862296392072300712)
XLA Ops:
  1.3 0.7 pad.15.want_ref
  2.0 0.1 pad.19.clone
  2.0 0.1 pad.22.clone
  2.1 0.1 add_add_fusion.1
  2.2 0.7 pad_bitcast_fusion
  2.9 0.7 pad_add_fusion
  3.6 0.1 select_reduce_fusion
  3.7 0.1 add_add_fusion.meta_ref
  3.8 1.1 reshape.31
  4.9 0.2 copy.11
  5.1 0.0 copy-start
  5.1 1.4 copy-done
  6.5 194.3 %apply_all.1 = (f32[256,256]{1,0:T(8,128)S(1)}, f32[256,256]{1,0:T(8,128)S(1)}) custom-call(bf16[48,128,128]{2,1,0:T(8,128)(2,1)S(1)} %bitcast.12, bf16[4,2,64,128]{3,2,1,0:T(8,128)(2,1)S(1)} %bitcast.13, s32[8,128]{1,0:T(8,128)S(1)} %add_add_fusion.meta_ref, s32[1,128]{1,0:T(1,128)S(1)} %pad.15.want_ref), custom_call_target="tpu_custom_call" | custom-call | tf_op jit(solution)/shard_map/apply_all/pallas_call | solution.py:525
  200.8 0.7 copy.17
  201.5 0.7 copy.18
  (7 shorter events, 0.0 us)
Async XLA Ops:
  5.1 1.4 copy-start

commit v3 on v1

--- a/solution.py
+++ b/solution.py
@@ -14,30 +14,34 @@
 SLOT, ROW, PREV_ROW, PREV_SLOT, LAST_ROW, LAST_SLOT = range(6)
 
 
-def chains(tile_row, tile_slot, tile_count):
-    total = tile_row.shape[0]
-    order = jnp.arange(total, dtype=jnp.int32)
-    live = order < tile_count
-    lane = jnp.arange(LANES, dtype=jnp.int32)
-    pad = lambda values: jnp.pad(values, (0, LANES - total))
-    keys = jnp.stack([tile_row, tile_slot, tile_row, tile_slot])
-    query = jnp.stack([pad(tile_row), pad(tile_slot), lane, lane])
-    bound = jnp.stack([lane, lane, jnp.full_like(lane, total), jnp.full_like(lane, total)])
-    hit = (keys[:, None, :] == query[:, :, None]) & live & (order < bound[:, :, None])
-    found = jnp.max(jnp.where(hit, order + 1, 0), axis=2)
-    head = jnp.stack([pad(tile_slot), pad(tile_row)])
-    return jnp.concatenate([head, found, jnp.zeros((2, LANES), jnp.int32)], axis=0)
+def chains(rows, slots, count, meta):
+    shape = (LANES, LANES)
+    earlier = lax.broadcasted_iota(jnp.int32, shape, 0)
+    lane = lax.broadcasted_iota(jnp.int32, shape, 1)
+    live = earlier < count
+    lane_value = lane.astype(jnp.float32)
+    for key, prev_key, last_key, values in ((ROW, PREV_ROW, LAST_ROW, rows), (SLOT, PREV_SLOT, LAST_SLOT, slots)):
+        across = jnp.broadcast_to(values.astype(jnp.float32), shape)
+        down = across.T
+        meta[key:key + 1] = values
+        hit = live & (earlier < lane) & (across == down)
+        meta[prev_key:prev_key + 1] = jnp.max(jnp.where(hit, earlier + 1, 0), axis=0, keepdims=True)
+        hit = live & (lane_value == down)
+        meta[last_key:last_key + 1] = jnp.max(jnp.where(hit, earlier + 1, 0), axis=0, keepdims=True)
 
 
 def apply_kernel(
     n_rows, n_grp, slots, chunks,
-    tiles_ref, omega_ref, meta_ref, want_ref, out_ref,
+    tiles_ref, row_ref, slot_ref, count_ref, want_ref, omega_ref, basis_ref, factor_ref,
+    row_v, slot_v, count_v, want_v, omega_v, keys, omega_parts,
     tbuf, meta_all, meta_s, want_all, want_s, prev_v, prev_s, last_v, last_s,
     omega_all, ghosts, ghost_out, partial, z_blocks,
     contrib_out, contrib_in, w_partial, w_blocks, w_ghosts, w_ghost_out, y_blocks, y_in,
-    local_sem, small_send, small_recv, omega_send, omega_recv, want_send, want_recv,
+    y_all, gram_out, gram_in, row_out, row_in, gram_all, work,
+    in_sem, local_sem, small_send, small_recv, omega_send, omega_recv, want_send, want_recv,
     right_send, right_recv, left_send, left_recv, fwd_send, fwd_recv,
     ghost_send, ghost_recv, contrib_send, contrib_recv, wg_send, wg_recv, y_send, y_recv,
+    gram_send, gram_recv, row_send, row_recv, all_send, all_recv,
 ):
     me = lax.axis_index("rows")
     grp = lax.axis_index("grp")
@@ -56,7 +60,49 @@
     for step in range(1, n_grp):
         pl.semaphore_signal(barrier, inc=1, device_id={"grp": group(step)}, device_id_type=MESH)
     lax.fori_loop(1, n_rows, greet, 0)
-    pl.semaphore_wait(barrier, n_rows - 1 + n_grp - 1)
+    inner = gram_out.shape[1]
+    spot = lax.rem(me, inner)
+    level = lax.div(me, inner)
+
+    def near(far, step):
+        return {"rows": level * inner + lax.rem(spot + step, inner), "grp": lax.rem(grp + far, n_grp)}
+
+    def greet_near(step, carry):
+        for far in range(1, n_grp):
+            pl.semaphore_signal(barrier, inc=1, device_id=near(far, step), device_id_type=MESH)
+        return carry
+
+    lax.fori_loop(1, inner, greet_near, 0)
+
+    brought = [
+        pltpu.make_async_copy(src, dst, in_sem.at[i])
+        for i, (src, dst) in enumerate(
+            ((omega_ref, omega_v), (row_ref, row_v), (slot_ref, slot_v), (count_ref, count_v), (want_ref, want_v)))
+    ]
+    own_tiles = pltpu.make_async_copy(tiles_ref.at[0, 0], tbuf.at[0], local_sem.at[0])
+    for copy in brought:
+        copy.start()
+    own_tiles.start()
+    keys[...] = jnp.zeros(keys.shape, jnp.int32)
+    partial[:, 0] = jnp.zeros((n_grp,) + partial.shape[2:], jnp.float32)
+    w_partial[0] = jnp.zeros(w_partial.shape[1:], jnp.float32)
+    for copy in brought:
+        copy.wait()
+    keys[0:1, :slots] = row_v[0]
+    keys[1:2, :slots] = slot_v[0]
+    keys[2:3, :n_rows] = want_v[...]
+    meta_all[0] = jnp.zeros(meta_all.shape[1:], jnp.int32)
+    chains(keys[0:1], keys[1:2], count_v[...], meta_all.at[0])
+    want_all[me] = keys[2:3]
+    width = omega_parts.shape[2]
+    turned = omega_v[...].astype(jnp.float32).T.astype(jnp.bfloat16)
+    for g in range(n_grp):
+        for j in range(owned):
+            omega_parts[g, j] = turned[g * width:(g + 1) * width, j * LANES:(j + 1) * LANES]
+    for j in range(owned):
+        omega_all[grp * owned + j] = omega_parts[grp, j]
+
+    pl.semaphore_wait(barrier, n_rows - 1 + (n_grp - 1) * inner)
 
     def over_x(src, dst, send, recv, to):
         return pltpu.make_async_remote_copy(
@@ -67,25 +113,25 @@
             src_ref=src, dst_ref=dst, send_sem=send, recv_sem=recv, device_id={"rows": to}, device_id_type=MESH)
 
     def want_copy(step):
-        return over_rows(want_ref, want_all.at[me], want_send.at[step], want_recv.at[step], peer(step))
+        return over_rows(keys.at[pl.ds(2, 1)], want_all.at[me], want_send.at[step], want_recv.at[step], peer(step))
 
     def want_arrival(step):
         came = lax.rem(me - step + n_rows, n_rows)
-        return over_rows(want_ref, want_all.at[came], want_send.at[step], want_recv.at[step], peer(step))
+        return over_rows(keys.at[pl.ds(2, 1)], want_all.at[came], want_send.at[step], want_recv.at[step], peer(step))
 
     def meta_copy(step):
         place = (0, 1, 3, 2)[step]
-        return over_x(meta_ref, meta_all.at[place], small_send.at[step], small_recv.at[step], group(step))
+        return over_x(meta_all.at[0], meta_all.at[place], small_send.at[step], small_recv.at[step], group(step))
 
     def omega_copy(step):
         to = group(step)
         return over_x(
-            omega_ref.at[to], omega_all.at[pl.ds(grp * owned, owned)], omega_send.at[step], omega_recv.at[step], to)
+            omega_parts.at[to], omega_all.at[pl.ds(grp * owned, owned)], omega_send.at[step], omega_recv.at[step], to)
 
     def omega_arrival(step):
         came = group(n_grp - step)
         return over_x(
-            omega_ref.at[came], omega_all.at[pl.ds(came * owned, owned)], omega_send.at[step], omega_recv.at[step], came)
+            omega_parts.at[came], omega_all.at[pl.ds(came * owned, owned)], omega_send.at[step], omega_recv.at[step], came)
 
     def start_want(step, carry):
         want_copy(step).start()
@@ -96,16 +142,13 @@
         omega_copy(step).start()
         meta_copy(step).start()
 
-    own_tiles = pltpu.make_async_copy(tiles_ref, tbuf.at[0], local_sem.at[0])
-    own_tiles.start()
-
     def to_right(c):
         part = pl.ds(c * per, per)
-        return over_x(tiles_ref.at[part], tbuf.at[1, part], right_send.at[c], right_recv.at[c], right)
+        return over_x(tiles_ref.at[0, 0, part], tbuf.at[1, part], right_send.at[c], right_recv.at[c], right)
 
     def to_left(c):
         part = pl.ds(c * per, per)
-        return over_x(tiles_ref.at[part], tbuf.at[2, part], left_send.at[c], left_recv.at[c], left)
+        return over_x(tiles_ref.at[0, 0, part], tbuf.at[2, part], left_send.at[c], left_recv.at[c], left)
 
     def forward(c):
         part = pl.ds(c * per, per)
@@ -117,12 +160,6 @@
         to_right(c).start()
         to_left(c).start()
 
-    want_all[me] = want_ref[...]
-    for j in range(owned):
-        omega_all[grp * owned + j] = omega_ref[grp, j]
-    meta_all[0] = meta_ref[...]
-    partial[:, 0] = jnp.zeros((n_grp,) + partial.shape[2:], jnp.float32)
-    w_partial[0] = jnp.zeros(w_partial.shape[1:], jnp.float32)
 
     def wait_want(step, carry):
         want_arrival(step).wait_recv()
@@ -295,11 +332,78 @@
         y_in[0, j] = y_blocks[grp * owned + j]
     for step in range(1, n_grp):
         y_copy(step).wait_recv()
-    width = out_ref.shape[0] // n_grp
     for step in range(n_grp):
-        came = group(n_grp - step) if step else grp
+        came = group(n_grp - step)
         for j in range(owned):
-            out_ref[pl.ds(pl.multiple_of(came * width, width), width), pl.ds(j * LANES, LANES)] = y_in[step, j]
+            y_all[pl.ds(pl.multiple_of(came * width, width), width), pl.ds(j * LANES, LANES)] = y_in[step, j]
+
+    outer = n_rows // inner
+    y_value = y_all[...]
+    own_gram = lax.dot_general(
+        y_value, y_value, (((1,), (1,)), ((), ())), precision=lax.Precision.HIGHEST, preferred_element_type=jnp.float32)
+    gram_out[...] = own_gram.reshape(gram_out.shape)
+
+    def to_near(src, dst, send, recv, far, step):
+        return pltpu.make_async_remote_copy(
+            src_ref=src, dst_ref=dst, send_sem=send.at[far, step], recv_sem=recv.at[far, step],
+            device_id=near(far, step), device_id_type=MESH)
+
+    def gram_copy(far, step):
+        return to_near(
+            gram_out.at[group(far), lax.rem(spot + step, inner)], gram_in.at[grp, spot], gram_send, gram_recv, far, step)
+
+    def gram_arrival(far, step):
+        came = (group(n_grp - far), lax.rem(spot + inner - step, inner))
+        return to_near(gram_out.at[came], gram_in.at[came], gram_send, gram_recv, far, step)
+
+    def all_copy(far, step):
+        return to_near(gram_all.at[grp, spot], gram_all.at[grp, spot], all_send, all_recv, far, step)
+
+    def all_arrival(far, step):
+        came = (group(n_grp - far), lax.rem(spot + inner - step, inner))
+        return to_near(gram_all.at[came], gram_all.at[came], all_send, all_recv, far, step)
+
+    def every_near(act):
+        for far in (2, 1, 3, 0):
+            def one(step, carry, far=far):
+                act(far, step)
+                return carry
+            lax.fori_loop(1 if far == 0 else 0, inner, one, 0)
+
+    every_near(lambda far, step: gram_copy(far, step).start())
+    gram_in[grp, spot] = gram_out[grp, spot]
+    every_near(lambda far, step: gram_arrival(far, step).wait_recv())
+    row_out[...] = jnp.sum(gram_in[...], axis=(0, 1))
+
+    def across(step):
+        return lax.rem(level + step, outer)
+
+    def row_copy(step):
+        return over_rows(
+            row_out, row_in.at[level], row_send.at[step], row_recv.at[step], across(step) * inner + spot)
+
+    def row_arrival(step):
+        came = across(outer - step)
+        return over_rows(row_out, row_in.at[came], row_send.at[step], row_recv.at[step], came * inner + spot)
+
+    for step in range(1, outer):
+        row_copy(step).start()
+    row_in[level] = row_out[...]
+    for step in range(1, outer):
+        row_arrival(step).wait_recv()
+    gram_all[grp, spot] = jnp.sum(row_in[...], axis=0)
+    every_near(lambda far, step: all_copy(far, step).start())
+    every_near(lambda far, step: all_arrival(far, step).wait_recv())
+
+    scale = math.sqrt(n_rows * RBD * LANES)
+    order = work.shape[0]
+    eliminate(gram_all[...].reshape(order, order), work)
+    place_row = lax.broadcasted_iota(jnp.int32, (order, order), 0)
+    place_col = lax.broadcasted_iota(jnp.int32, (order, order), 1)
+    factor_ref[...] = jnp.where(place_col >= place_row, work[:, :order], 0.0) * (1.0 / scale)
+    solved = jnp.dot(
+        work[:, order:], y_value, precision=lax.Precision.HIGHEST, preferred_element_type=jnp.float32)
+    basis_ref[...] = solved.T * scale
 
     def drain(step, carry):
         want_copy(step).wait_send()
@@ -313,21 +417,95 @@
         meta_copy(step).wait_send()
         omega_copy(step).wait_send()
         y_copy(step).wait_send()
+    every_near(lambda far, step: gram_copy(far, step).wait_send())
+    every_near(lambda far, step: all_copy(far, step).wait_send())
+    for step in range(1, outer):
+        row_copy(step).wait_send()
     for c in range(chunks):
         to_right(c).wait_send()
         to_left(c).wait_send()
         forward(c).wait_send()
 
 
-def apply_all(tiles, omega_parts, meta, want_row, n_rows, n_grp, chunks):
-    slots, tile, _ = tiles.shape
+BLOCK = 64
+EIGHT = 8
+
+
+def invert_factor(matrix):
+    size = matrix.shape[0]
+    groups = size // EIGHT
+    place_row = lax.broadcasted_iota(jnp.int32, (size, size), 0)
+    place_col = lax.broadcasted_iota(jnp.int32, (size, size), 1)
+    both = jnp.concatenate([matrix, jnp.where(place_row == place_col, 1.0, 0.0)], axis=1)
+    rows = [both[EIGHT * r:EIGHT * (r + 1)] for r in range(groups)]
+    spread = lambda values: jnp.broadcast_to(values, (EIGHT, 2 * size))
+    within = lax.broadcasted_iota(jnp.int32, (EIGHT, 2 * size), 0)
+    pivots = []
+    for s in range(groups):
+        columns = [
+            [spread(rows[r][:, EIGHT * s + j:EIGHT * s + j + 1]) for j in range(EIGHT)] for r in range(s, groups)]
+        kept = jnp.ones((EIGHT, 2 * size), jnp.float32)
+        for k in range(EIGHT):
+            pivot = spread(columns[0][k][k:k + 1])
+            kept = jnp.where(within == k, pivot, kept)
+            inverse = 1.0 / pivot
+            ratio = [column[k] * inverse for column in columns]
+            ratio[0] = jnp.where(within > k, ratio[0], 0.0)
+            for j in range(k + 1, EIGHT):
+                entry = spread(columns[0][j][k:k + 1])
+                for r in range(groups - s):
+                    columns[r][j] = columns[r][j] - ratio[r] * entry
+            entry = spread(rows[s][k:k + 1])
+            for r in range(groups - s):
+                rows[s + r] = rows[s + r] - ratio[r] * entry
+        pivots.append(kept)
+    scaled = jnp.concatenate([rows[r] * lax.rsqrt(pivots[r]) for r in range(groups)], axis=0)
+    return scaled[:, size:]
+
+
+def eliminate(gram, work):
+    order = gram.shape[0]
+    work[:, :order] = gram
+    place_row = lax.broadcasted_iota(jnp.int32, (order, order), 0)
+    place_col = lax.broadcasted_iota(jnp.int32, (order, order), 1)
+    work[:, order:] = jnp.where(place_row == place_col, 1.0, 0.0)
+    for first in range(0, order, BLOCK):
+        after = first + BLOCK
+        low = first // LANES * LANES
+        high = order + low + LANES
+        inverse = invert_factor(work[first:after, first:after])
+        done = jnp.dot(
+            inverse, work[first:after, low:high], precision=lax.Precision.HIGHEST, preferred_element_type=jnp.float32)
+        work[first:after, low:high] = done
+        if after < order:
+            work[after:, low:high] = work[after:, low:high] - lax.dot_general(
+                done[:, after - low:order - low], done, (((0,), (0,)), ((), ())),
+                precision=lax.Precision.HIGHEST, preferred_element_type=jnp.float32)
+
+
+def per_device(tiles, tile_row, tile_slot, tile_count, want, omega):
+    slots, tile = tiles.shape[2], tiles.shape[-1]
+    order = omega.shape[1]
+    n_rows = lax.axis_size("rows")
+    n_grp = lax.axis_size("grp")
+    chunks = 8 if slots % 8 == 0 and slots >= 48 else 2
     owned = RBD // n_grp
-    width = omega_parts.shape[2]
+    width = order // n_grp
     block = (width, tile)
+    inner = 8 if n_rows % 8 == 0 else n_rows
+    some = width // inner
     bf16, f32, i32 = jnp.bfloat16, jnp.float32, jnp.int32
     dma = lambda count: pltpu.SemaphoreType.DMA((count,))
+    near = pltpu.SemaphoreType.DMA((n_grp, inner))
     vmem = pl.BlockSpec(memory_space=pltpu.VMEM)
     scratch = [
+        pltpu.VMEM((1, 1, slots), i32),
+        pltpu.VMEM((1, 1, slots), i32),
+        pltpu.VMEM((1, 1), i32),
+        pltpu.VMEM((1, n_rows), i32),
+        pltpu.VMEM((order, order), bf16),
+        pltpu.VMEM((8, LANES), i32),
+        pltpu.VMEM((n_grp, owned) + block, bf16),
         pltpu.VMEM((n_grp, slots, tile, tile), bf16),
         pltpu.VMEM((n_grp, 8, LANES), i32),
         pltpu.SMEM((n_grp, 8, LANES), i32),
@@ -350,44 +528,31 @@
         pltpu.VMEM((n_rows,) + block, bf16),
         pltpu.VMEM((RBD,) + block, f32),
         pltpu.VMEM((n_grp, owned) + block, f32),
-        dma(3), dma(n_grp), dma(n_grp), dma(n_grp), dma(n_grp), dma(n_rows), dma(n_rows),
+        pltpu.VMEM((order, owned * tile), f32),
+        pltpu.VMEM((n_grp, inner, some, order), f32),
+        pltpu.VMEM((n_grp, inner, some, order), f32),
+        pltpu.VMEM((some, order), f32),
+        pltpu.VMEM((n_rows // inner, some, order), f32),
+        pltpu.VMEM((n_grp, inner, some, order), f32),
+        pltpu.VMEM((order, 2 * order), f32),
+        dma(5), dma(3), dma(n_grp), dma(n_grp), dma(n_grp), dma(n_grp), dma(n_rows), dma(n_rows),
         dma(chunks), dma(chunks), dma(chunks), dma(chunks), dma(chunks), dma(chunks),
         dma(n_rows), dma(n_rows), dma(n_rows), dma(n_rows), dma(n_rows), dma(n_rows), dma(n_grp), dma(n_grp),
+        near, near, dma(n_rows // inner), dma(n_rows // inner), near, near,
     ]
     return pl.pallas_call(
         functools.partial(apply_kernel, n_rows, n_grp, slots, chunks),
-        out_shape=jax.ShapeDtypeStruct((width * n_grp, owned * tile), f32),
-        in_specs=[pl.BlockSpec(memory_space=pl.ANY), vmem, vmem, vmem],
-        out_specs=vmem,
+        out_shape=(
+            jax.ShapeDtypeStruct((owned * tile, order), f32),
+            jax.ShapeDtypeStruct((order, order), f32),
+        ),
+        in_specs=[pl.BlockSpec(memory_space=pl.ANY)] * 6,
+        out_specs=(vmem, vmem),
         scratch_shapes=scratch,
         compiler_params=pltpu.CompilerParams(
             collective_id=0, has_side_effects=True, vmem_limit_bytes=40 * 1024 * 1024),
         name="apply_all",
-    )(tiles, omega_parts, meta, want_row)
-
-
-def per_device(tiles, tile_row, tile_slot, tile_count, want, omega):
-    tile = tiles.shape[-1]
-    slots = tiles.shape[2]
-    columns = omega.shape[1]
-    n_rows = lax.axis_size("rows")
-    n_grp = lax.axis_size("grp")
-    highest = lax.Precision.HIGHEST
-    chunks = 8 if slots % 8 == 0 and slots >= 48 else 2
-    owned = RBD // n_grp
-    meta = chains(tile_row.reshape(slots), tile_slot.reshape(slots), tile_count.reshape(()))
-    want_row = jnp.pad(want.reshape(1, n_rows), ((0, 0), (0, LANES - n_rows)))
-    omega_parts = omega.reshape(owned, tile, n_grp, columns // n_grp).transpose(2, 0, 3, 1)
-    y_t = apply_all(tiles.reshape(slots, tile, tile), omega_parts, meta, want_row, n_rows, n_grp, chunks)
-    partial_gram = lax.dot_general(
-        y_t, y_t, (((1,), (1,)), ((), ())), precision=highest, preferred_element_type=jnp.float32)
-    gram = lax.psum(lax.psum(partial_gram, "grp"), "rows")
-    factor_low = jnp.linalg.cholesky(gram)
-    norm_scale = math.sqrt(n_rows * RBD * tile)
-    basis = (
-        lax.linalg.triangular_solve(factor_low, y_t.T, left_side=False, lower=True, transpose_a=True) * norm_scale
-    )
-    return (basis, factor_low.T / norm_scale)
+    )(tiles, tile_row, tile_slot, tile_count, want, omega)
 
 
 def solution(mesh):

time: 456 us -> 182 us (0.40)
  waiting for transfers between devices: 225 us -> 0 us
  other arithmetic: 56.4 us -> 0 us
  Pallas kernels: 144 us -> 175 us
  between operations: 16.2 us -> 1.3 us
  local copies, waits for them, and re-layouts: 11.1 us -> 5.68 us
    psum x2 -> x0, waiting for transfers between devices: 225 us -> none  [per_device(): gram = lax.psum(lax.psum(partial_gram, 'grp'), 'rows')]
    another operation x12 -> x0, other arithmetic: 55.2 us -> none  [the longest x7 34.7 us: per_device(): factor_low = jnp.linalg.cholesky(gram)]
    pallas_call x1, Pallas kernels: 144 us -> 175 us  [per_device(): pl.pallas_call(functools.partial(apply_kernel, n_rows, n_grp, slots, chun...]
    another operation x12 -> x0, local copies, waits for them, and re-layouts: 4.91 us -> none
  transfers between devices with their start and end apart: 2 -> 0, of which waited for: 2 -> 0; matrix products, arithmetic and copies ran while one was open for 0% -> 0% of each run, Pallas kernels for 0% -> 0%
where the time goes in v3:
time: 182 us
  Pallas kernels  175 us (96%)
  local copies, waits for them, and re-layouts  5.68 us (3%)
    pallas_call x1, Pallas kernels, per_device(): pl.pallas_call(functools.partial(apply_kernel, n_rows, n_grp, slots, chun...  175 us
    unnamed x12, local copies, waits for them, and re-layouts  5.68 us

profile of v3, /device:TPU:1, one launch (start us, length us, event | category | flops | bytes accessed | tf_op | source)
XLA Modules:
  0.0 182.1 jit_solution(13998303240523031387)
XLA Ops:
  1.3 0.0 copy-start
  1.3 1.4 copy-done
  2.7 0.0 copy-start.1
  2.7 0.9 copy-done.1
  3.6 0.0 copy-start.2
  3.6 0.7 copy-done.2
  4.2 0.0 copy-start.3
  4.2 0.7 copy-done.3
  4.9 0.0 copy-start.4
  4.9 0.7 copy-done.4
  5.6 175.2 %apply_all.1 = (f32[256,256]{1,0:T(8,128)S(1)}, f32[256,256]{1,0:T(8,128)S(1)}) custom-call(bf16[1,1,48,128,128]{4,3,2,1,0:T(8,128)(2,1)S(1)} %copy-done, s32[1,1,48]{2,1,0:T(1,128)S(1)} %copy-done.2, s32[1,1,48]{2,1,0:T(1,128)S(1)} %copy-done.3, s32[1,1]{1,0:T(1,128)S(6)} %copy.10.count_ref, s32[1,64]{1,0:T(1,128)S(1)} %copy-done.4, ...), custom_call_target="tpu_custom_call" | custom-call | tf_op jit(solution)/shard_map/apply_all/pallas_call | solution.py:543
  180.7 0.7 copy.11
  181.4 0.7 copy.12
Async XLA Ops:
  1.3 1.4 copy-start
  2.7 0.9 copy-start.1
  3.6 0.7 copy-start.2
  4.2 0.7 copy-start.3
  4.9 0.7 copy-start.4

commit v4 on v3

--- a/solution.py
+++ b/solution.py
@@ -9,6 +9,7 @@
 from jax.sharding import PartitionSpec as P
 
 RBD = 8
+MANY = 48
 LANES = 128
 MESH = pl.DeviceIdType.MESH
 SLOT, ROW, PREV_ROW, PREV_SLOT, LAST_ROW, LAST_SLOT = range(6)
@@ -36,12 +37,12 @@
     row_v, slot_v, count_v, want_v, omega_v, keys, omega_parts,
     tbuf, meta_all, meta_s, want_all, want_s, prev_v, prev_s, last_v, last_s,
     omega_all, ghosts, ghost_out, partial, z_blocks,
-    contrib_out, contrib_in, w_partial, w_blocks, w_ghosts, w_ghost_out, y_blocks, y_in,
-    y_all, gram_out, gram_in, row_out, row_in, gram_all, work,
-    in_sem, local_sem, small_send, small_recv, omega_send, omega_recv, want_send, want_recv,
+    contrib_out, contrib_in, w_partial, w_blocks, w_ghosts_0, w_ghosts_1, w_ghost_out, y_blocks, y_in,
+    y_all, gram_whole, gram_out, gram_in, row_out, row_in, gram_all, work,
+    in_sem, local_sem, small_send, small_recv, omega_send, omega_recv, want_sem,
     right_send, right_recv, left_send, left_recv, fwd_send, fwd_recv,
-    ghost_send, ghost_recv, contrib_send, contrib_recv, wg_send, wg_recv, y_send, y_recv,
-    gram_send, gram_recv, row_send, row_recv, all_send, all_recv,
+    ghost_sem, contrib_sem, wg_sem, y_send, y_recv,
+    gram_sem, row_send, row_recv, all_sem,
 ):
     me = lax.axis_index("rows")
     grp = lax.axis_index("grp")
@@ -60,7 +61,7 @@
     for step in range(1, n_grp):
         pl.semaphore_signal(barrier, inc=1, device_id={"grp": group(step)}, device_id_type=MESH)
     lax.fori_loop(1, n_rows, greet, 0)
-    inner = gram_out.shape[1]
+    inner = gram_out.shape[0] // n_grp
     spot = lax.rem(me, inner)
     level = lax.div(me, inner)
 
@@ -93,7 +94,7 @@
     keys[2:3, :n_rows] = want_v[...]
     meta_all[0] = jnp.zeros(meta_all.shape[1:], jnp.int32)
     chains(keys[0:1], keys[1:2], count_v[...], meta_all.at[0])
-    want_all[me] = keys[2:3]
+    want_all[0] = keys[2:3]
     width = omega_parts.shape[2]
     turned = omega_v[...].astype(jnp.float32).T.astype(jnp.bfloat16)
     for g in range(n_grp):
@@ -112,12 +113,31 @@
         return pltpu.make_async_remote_copy(
             src_ref=src, dst_ref=dst, send_sem=send, recv_sem=recv, device_id={"rows": to}, device_id_type=MESH)
 
+    peers = n_rows - 1
+
+    def to_peers(buffer_out, buffer_in, sems):
+        def copy(step):
+            return over_rows(buffer_out.at[step], buffer_in.at[step], sems.at[0], sems.at[1], peer(step))
+
+        def arrived():
+            whole = buffer_in.at[pl.ds(1, peers)]
+            pltpu.make_async_copy(whole, whole, sems.at[1]).wait()
+
+        def sent():
+            whole = buffer_out.at[pl.ds(1, peers)]
+            pltpu.make_async_copy(whole, whole, sems.at[0]).wait()
+
+        return copy, arrived, sent
+
+    def each_peer(act):
+        few = 7
+        def body(i, carry):
+            act([1 + i * few + j for j in range(few)])
+            return carry
+        lax.fori_loop(0, peers // few, body, 0)
+
     def want_copy(step):
-        return over_rows(keys.at[pl.ds(2, 1)], want_all.at[me], want_send.at[step], want_recv.at[step], peer(step))
-
-    def want_arrival(step):
-        came = lax.rem(me - step + n_rows, n_rows)
-        return over_rows(keys.at[pl.ds(2, 1)], want_all.at[came], want_send.at[step], want_recv.at[step], peer(step))
+        return over_rows(keys.at[pl.ds(2, 1)], want_all.at[step], want_sem.at[0], want_sem.at[1], peer(step))
 
     def meta_copy(step):
         place = (0, 1, 3, 2)[step]
@@ -133,11 +153,11 @@
         return over_x(
             omega_parts.at[came], omega_all.at[pl.ds(came * owned, owned)], omega_send.at[step], omega_recv.at[step], came)
 
-    def start_want(step, carry):
-        want_copy(step).start()
-        return carry
-
-    lax.fori_loop(1, n_rows, start_want, 0)
+    def start_want(steps):
+        for step in steps:
+            want_copy(step).start()
+
+    each_peer(start_want)
     for step in range(1, n_grp):
         omega_copy(step).start()
         meta_copy(step).start()
@@ -161,11 +181,8 @@
         to_left(c).start()
 
 
-    def wait_want(step, carry):
-        want_arrival(step).wait_recv()
-        return carry
-
-    lax.fori_loop(1, n_rows, wait_want, 0)
+    want_part = want_all.at[pl.ds(1, peers)]
+    pltpu.make_async_copy(want_part, want_part, want_sem.at[1]).wait()
     want_down = pltpu.make_async_copy(want_all, want_s, local_sem.at[1])
     want_down.start()
     for step in range(1, n_grp):
@@ -176,21 +193,22 @@
     want_down.wait()
     meta_down.wait()
 
-    def ghost_copy(step):
-        return over_rows(ghost_out.at[step], ghosts.at[step], ghost_send.at[step], ghost_recv.at[step], peer(step))
-
-    def start_ghost(step, carry):
-        ghost_out[step] = omega_all[want_s[peer(step), 0, me]]
-        ghost_copy(step).start()
-        return carry
-
-    ghosts[0] = omega_all[want_s[me, 0, me]]
-    lax.fori_loop(1, n_rows, start_ghost, 0)
+    ghost_copy, ghosts_arrived, ghosts_sent = to_peers(ghost_out, ghosts, ghost_sem)
+
+    def start_ghosts(steps):
+        blocks = [omega_all[want_s[n_rows - step, 0, me]] for step in steps]
+        for step, block in zip(steps, blocks):
+            ghost_out[step] = block
+        for step in steps:
+            ghost_copy(step).start()
+
+    ghosts[0] = omega_all[want_s[0, 0, me]]
+    each_peer(start_ghosts)
 
     blocks = lax.broadcasted_iota(jnp.int32, (RBD, LANES), 0)
 
     def link(step, last):
-        row = want_all[lax.rem(me - step + n_rows, n_rows)]
+        row = want_all[step]
         hit = blocks == row
         prev_v[step] = jnp.max(jnp.where(hit, last, 0), axis=0, keepdims=True)
         return jnp.where(hit, step + 1, last)
@@ -212,114 +230,108 @@
         if c >= chunks // 2:
             forward(c).start()
 
-    def wait_ghost(step, carry):
-        ghost_copy(step).wait_recv()
-        return carry
-
-    lax.fori_loop(1, n_rows, wait_ghost, 0)
-
-    unroll = per
-
-    def multiply(place, first, source, by_row, sent):
-        prev_key = PREV_ROW if by_row else PREV_SLOT
+    ghosts_arrived()
+
+    half = partial.shape[3]
+    halves = range(partial.shape[2])
+    w_ghosts = (w_ghosts_0, w_ghosts_1)
+
+    def chunk_z(place, first, count):
         products = []
-        for i in range(unroll):
-            t = first + i
-            tile = tbuf[place, t]
-            if by_row:
-                slot = meta_s[place, SLOT, t]
-                block = source[lax.rem(me - slot + n_rows, n_rows)]
-                product = lax.dot_general(block, tile, (((1,), (1,)), ((), ())), preferred_element_type=jnp.float32)
-            else:
-                block = source[meta_s[place, ROW, t]]
-                product = lax.dot_general(block, tile, (((1,), (0,)), ((), ())), preferred_element_type=jnp.float32)
-            products.append(product)
-        for i in range(unroll):
-            t = first + i
-            partial[place, t + 1] = products[i] + partial[place, meta_s[place, prev_key, t]]
-
-    def whole(place, source, by_row):
-        def step(c, carry):
-            multiply(place, c * unroll, source, by_row, None)
-            return carry
-        lax.fori_loop(0, slots // unroll, step, 0)
-
-    def total(key, index):
-        value = partial[0, meta_s[0, key, index]]
-        for place in range(1, n_grp):
-            value = value + partial[place, meta_s[place, key, index]]
-        return value
-
-    for place in range(3):
-        whole(place, ghosts, True)
+        for i in range(count):
+            block = ghosts[lax.rem(me - meta_s[place, SLOT, first + i] + n_rows, n_rows)]
+            products.append(lax.dot_general(
+                block, tbuf[place, first + i], (((1,), (1,)), ((), ())), preferred_element_type=jnp.float32))
+        for i in range(count):
+            before = partial[place, meta_s[place, PREV_ROW, first + i]]
+            partial[place, first + i + 1] = products[i].reshape(before.shape) + before
+
+    def chunk_w(place, first, count, h):
+        products = []
+        for i in range(count):
+            block = z_blocks[meta_s[place, ROW, first + i], h]
+            products.append(jnp.dot(block, tbuf[place, first + i], preferred_element_type=jnp.float32))
+        for i in range(count):
+            partial[place, first + i + 1, h] = (
+                products[i] + partial[place, meta_s[place, PREV_SLOT, first + i], h])
+
+    def chunk_y(place, first, count, h):
+        products = []
+        for i in range(count):
+            block = w_ghosts[h][lax.rem(me - meta_s[place, SLOT, first + i] + n_rows, n_rows)]
+            products.append(lax.dot_general(
+                block, tbuf[place, first + i], (((1,), (1,)), ((), ())), preferred_element_type=jnp.float32))
+        for i in range(count):
+            partial[place, first + i + 1, h] = (
+                products[i] + partial[place, meta_s[place, PREV_ROW, first + i], h])
+
+    many = MANY if slots % MANY == 0 else per
+
+    def every_chunk(places, act):
+        for place in places:
+            def step(c, carry, place=place):
+                act(place, c * many, many)
+                return carry
+            lax.fori_loop(0, slots // many, step, 0)
+
+    every_chunk(range(3), chunk_z)
     for c in range(chunks):
         forward(c).wait_recv()
-        multiply(3, c * per, ghosts, True, None)
-
-    def close_z(b, carry):
-        z_blocks[b] = total(LAST_ROW, b).astype(jnp.bfloat16)
-        return carry
-
-    lax.fori_loop(0, RBD, close_z, 0)
-
-    for place in range(n_grp):
-        whole(place, z_blocks, False)
-
-    def contrib_copy(step):
-        return over_rows(
-            contrib_out.at[step], contrib_in.at[step], contrib_send.at[step], contrib_recv.at[step], peer(step))
-
-    contrib_in[0] = total(LAST_SLOT, me).astype(jnp.bfloat16)
-
-    def start_contrib(step, carry):
-        contrib_out[step] = total(LAST_SLOT, peer(step)).astype(jnp.bfloat16)
-        contrib_copy(step).start()
-        return carry
-
-    lax.fori_loop(1, n_rows, start_contrib, 0)
-
-    def add_contrib(step):
-        w_partial[step + 1] = contrib_in[step].astype(jnp.float32) + w_partial[prev_s[step, 0, me]]
-
-    add_contrib(0)
-
-    def take_contrib(step, carry):
-        contrib_copy(step).wait_recv()
-        add_contrib(step)
-        return carry
-
-    lax.fori_loop(1, n_rows, take_contrib, 0)
-
-    def close_w(b, carry):
-        w_blocks[b] = w_partial[last_s[b, me]].astype(jnp.bfloat16)
-        return carry
-
-    lax.fori_loop(0, RBD, close_w, 0)
-
-    def wg_copy(step):
-        return over_rows(w_ghost_out.at[step], w_ghosts.at[step], wg_send.at[step], wg_recv.at[step], peer(step))
-
-    def start_wg(step, carry):
-        w_ghost_out[step] = w_blocks[want_s[peer(step), 0, me]]
-        wg_copy(step).start()
-        return carry
-
-    def wait_wg(step, carry):
-        wg_copy(step).wait_recv()
-        return carry
-
-    w_ghosts[0] = w_blocks[want_s[me, 0, me]]
-    lax.fori_loop(1, n_rows, start_wg, 0)
-    lax.fori_loop(1, n_rows, wait_wg, 0)
-
-    for place in range(n_grp):
-        whole(place, w_ghosts, True)
-
-    def close_y(b, carry):
-        y_blocks[b] = total(LAST_ROW, b)
-        return carry
-
-    lax.fori_loop(0, RBD, close_y, 0)
+        chunk_z(3, c * per, per)
+    for b in range(RBD):
+        value = partial[0, meta_s[0, LAST_ROW, b]]
+        for place in range(1, n_grp):
+            value = value + partial[place, meta_s[place, LAST_ROW, b]]
+        z_blocks[b] = value.astype(jnp.bfloat16)
+
+    def total(key, index, h):
+        value = partial[0, meta_s[0, key, index], h]
+        for place in range(1, n_grp):
+            value = value + partial[place, meta_s[place, key, index], h]
+        return value
+
+    contribs = [to_peers(contrib_out.at[h], contrib_in.at[h], contrib_sem.at[h]) for h in halves]
+    w_trips = [to_peers(w_ghost_out.at[h], w_ghosts[h], wg_sem.at[h]) for h in halves]
+    for h in halves:
+        every_chunk(range(n_grp), lambda place, first, count: chunk_w(place, first, count, h))
+
+        def start_contribs(steps):
+            blocks = [total(LAST_SLOT, peer(step), h).astype(jnp.bfloat16) for step in steps]
+            for step, block in zip(steps, blocks):
+                contrib_out[h, step] = block
+            for step in steps:
+                contribs[h][0](step).start()
+
+        contrib_in[h, 0] = total(LAST_SLOT, me, h).astype(jnp.bfloat16)
+        each_peer(start_contribs)
+
+    for h in halves:
+        contribs[h][1]()
+
+        def add_contribs(steps):
+            for step in steps:
+                w_partial[step + 1] = contrib_in[h, step].astype(jnp.float32) + w_partial[prev_s[step, 0, me]]
+
+        add_contribs([0])
+        each_peer(add_contribs)
+        for b in range(RBD):
+            w_blocks[b] = w_partial[last_s[b, me]].astype(jnp.bfloat16)
+
+        def start_w(steps):
+            blocks = [w_blocks[want_s[n_rows - step, 0, me]] for step in steps]
+            for step, block in zip(steps, blocks):
+                w_ghost_out[h, step] = block
+            for step in steps:
+                w_trips[h][0](step).start()
+
+        w_ghosts[h][0] = w_blocks[want_s[0, 0, me]]
+        each_peer(start_w)
+
+    for h in halves:
+        w_trips[h][1]()
+        every_chunk(range(n_grp), lambda place, first, count: chunk_y(place, first, count, h))
+        for b in range(RBD):
+            y_blocks[b, pl.ds(h * half, half)] = total(LAST_ROW, b, h)
 
     def y_copy(step):
         to = group(step)
@@ -341,39 +353,41 @@
     y_value = y_all[...]
     own_gram = lax.dot_general(
         y_value, y_value, (((1,), (1,)), ((), ())), precision=lax.Precision.HIGHEST, preferred_element_type=jnp.float32)
-    gram_out[...] = own_gram.reshape(gram_out.shape)
-
-    def to_near(src, dst, send, recv, far, step):
+    gram_whole[...] = own_gram.reshape(gram_whole.shape)
+
+    others = n_grp * inner - 1
+
+    def to_near(src, dst, sems, far, step):
         return pltpu.make_async_remote_copy(
-            src_ref=src, dst_ref=dst, send_sem=send.at[far, step], recv_sem=recv.at[far, step],
+            src_ref=src, dst_ref=dst, send_sem=sems.at[0], recv_sem=sems.at[1],
             device_id=near(far, step), device_id_type=MESH)
 
+    def part(far, step):
+        return group(far) * inner + lax.rem(spot + step, inner)
+
     def gram_copy(far, step):
-        return to_near(
-            gram_out.at[group(far), lax.rem(spot + step, inner)], gram_in.at[grp, spot], gram_send, gram_recv, far, step)
-
-    def gram_arrival(far, step):
-        came = (group(n_grp - far), lax.rem(spot + inner - step, inner))
-        return to_near(gram_out.at[came], gram_in.at[came], gram_send, gram_recv, far, step)
+        at = far * inner + step
+        return to_near(gram_out.at[at], gram_in.at[at], gram_sem, far, step)
 
     def all_copy(far, step):
-        return to_near(gram_all.at[grp, spot], gram_all.at[grp, spot], all_send, all_recv, far, step)
-
-    def all_arrival(far, step):
-        came = (group(n_grp - far), lax.rem(spot + inner - step, inner))
-        return to_near(gram_all.at[came], gram_all.at[came], all_send, all_recv, far, step)
+        return to_near(gram_all.at[0], gram_all.at[far * inner + step], all_sem, far, step)
+
+    def wait_others(buffer, sem):
+        whole = buffer.at[pl.ds(1, others)]
+        pltpu.make_async_copy(whole, whole, sem).wait()
 
     def every_near(act):
         for far in (2, 1, 3, 0):
-            def one(step, carry, far=far):
+            for step in range(1 if far == 0 else 0, inner):
                 act(far, step)
-                return carry
-            lax.fori_loop(1 if far == 0 else 0, inner, one, 0)
-
+
+    gram_in[0] = gram_whole[part(0, 0)]
+    parts = [(far, step) for far in range(n_grp) for step in range(inner)]
+    for far, step in parts[1:]:
+        gram_out[far * inner + step] = gram_whole[part(far, step)]
     every_near(lambda far, step: gram_copy(far, step).start())
-    gram_in[grp, spot] = gram_out[grp, spot]
-    every_near(lambda far, step: gram_arrival(far, step).wait_recv())
-    row_out[...] = jnp.sum(gram_in[...], axis=(0, 1))
+    wait_others(gram_in, gram_sem.at[1])
+    row_out[...] = jnp.sum(gram_in[...], axis=0)
 
     def across(step):
         return lax.rem(level + step, outer)
@@ -391,13 +405,16 @@
     row_in[level] = row_out[...]
     for step in range(1, outer):
         row_arrival(step).wait_recv()
-    gram_all[grp, spot] = jnp.sum(row_in[...], axis=0)
+    gram_all[0] = jnp.sum(row_in[...], axis=0)
     every_near(lambda far, step: all_copy(far, step).start())
-    every_near(lambda far, step: all_arrival(far, step).wait_recv())
+    wait_others(gram_all, all_sem.at[1])
+    for far, step in parts:
+        came = group(n_grp - far) * inner + lax.rem(spot + inner - step, inner)
+        gram_whole[came] = gram_all[far * inner + step]
 
     scale = math.sqrt(n_rows * RBD * LANES)
     order = work.shape[0]
-    eliminate(gram_all[...].reshape(order, order), work)
+    eliminate(gram_whole[...].reshape(order, order), work)
     place_row = lax.broadcasted_iota(jnp.int32, (order, order), 0)
     place_col = lax.broadcasted_iota(jnp.int32, (order, order), 1)
     factor_ref[...] = jnp.where(place_col >= place_row, work[:, :order], 0.0) * (1.0 / scale)
@@ -405,20 +422,17 @@
         work[:, order:], y_value, precision=lax.Precision.HIGHEST, preferred_element_type=jnp.float32)
     basis_ref[...] = solved.T * scale
 
-    def drain(step, carry):
-        want_copy(step).wait_send()
-        ghost_copy(step).wait_send()
-        contrib_copy(step).wait_send()
-        wg_copy(step).wait_send()
-        return carry
-
-    lax.fori_loop(1, n_rows, drain, 0)
+    pltpu.make_async_copy(want_part, want_part, want_sem.at[0]).wait()
+    ghosts_sent()
+    for h in halves:
+        contribs[h][2]()
+        w_trips[h][2]()
     for step in range(1, n_grp):
         meta_copy(step).wait_send()
         omega_copy(step).wait_send()
         y_copy(step).wait_send()
-    every_near(lambda far, step: gram_copy(far, step).wait_send())
-    every_near(lambda far, step: all_copy(far, step).wait_send())
+    wait_others(gram_out, gram_sem.at[0])
+    wait_others(gram_all, all_sem.at[0])
     for step in range(1, outer):
         row_copy(step).wait_send()
     for c in range(chunks):
@@ -492,11 +506,12 @@
     owned = RBD // n_grp
     width = order // n_grp
     block = (width, tile)
+    split = (2, width // 2, tile)
     inner = 8 if n_rows % 8 == 0 else n_rows
     some = width // inner
     bf16, f32, i32 = jnp.bfloat16, jnp.float32, jnp.int32
     dma = lambda count: pltpu.SemaphoreType.DMA((count,))
-    near = pltpu.SemaphoreType.DMA((n_grp, inner))
+    both = pltpu.SemaphoreType.DMA((2, 2))
     vmem = pl.BlockSpec(memory_space=pltpu.VMEM)
     scratch = [
         pltpu.VMEM((1, 1, slots), i32),
@@ -518,27 +533,29 @@
         pltpu.VMEM((RBD,) + block, bf16),
         pltpu.VMEM((n_rows,) + block, bf16),
         pltpu.VMEM((n_rows,) + block, bf16),
-        pltpu.VMEM((n_grp, slots + 1) + block, f32),
-        pltpu.VMEM((RBD,) + block, bf16),
-        pltpu.VMEM((n_rows,) + block, bf16),
-        pltpu.VMEM((n_rows,) + block, bf16),
-        pltpu.VMEM((n_rows + 1,) + block, f32),
-        pltpu.VMEM((RBD,) + block, bf16),
-        pltpu.VMEM((n_rows,) + block, bf16),
-        pltpu.VMEM((n_rows,) + block, bf16),
+        pltpu.VMEM((n_grp, slots + 1) + split, f32),
+        pltpu.VMEM((RBD,) + split, bf16),
+        pltpu.VMEM((2, n_rows) + split[1:], bf16),
+        pltpu.VMEM((2, n_rows) + split[1:], bf16),
+        pltpu.VMEM((n_rows + 1,) + split[1:], f32),
+        pltpu.VMEM((RBD,) + split[1:], bf16),
+        pltpu.VMEM((n_rows,) + split[1:], bf16),
+        pltpu.VMEM((n_rows,) + split[1:], bf16),
+        pltpu.VMEM((2, n_rows) + split[1:], bf16),
         pltpu.VMEM((RBD,) + block, f32),
         pltpu.VMEM((n_grp, owned) + block, f32),
         pltpu.VMEM((order, owned * tile), f32),
-        pltpu.VMEM((n_grp, inner, some, order), f32),
-        pltpu.VMEM((n_grp, inner, some, order), f32),
+        pltpu.VMEM((n_grp * inner, some, order), f32),
+        pltpu.VMEM((n_grp * inner, some, order), f32),
+        pltpu.VMEM((n_grp * inner, some, order), f32),
         pltpu.VMEM((some, order), f32),
         pltpu.VMEM((n_rows // inner, some, order), f32),
-        pltpu.VMEM((n_grp, inner, some, order), f32),
+        pltpu.VMEM((n_grp * inner, some, order), f32),
         pltpu.VMEM((order, 2 * order), f32),
-        dma(5), dma(3), dma(n_grp), dma(n_grp), dma(n_grp), dma(n_grp), dma(n_rows), dma(n_rows),
+        dma(5), dma(3), dma(n_grp), dma(n_grp), dma(n_grp), dma(n_grp), dma(2),
         dma(chunks), dma(chunks), dma(chunks), dma(chunks), dma(chunks), dma(chunks),
-        dma(n_rows), dma(n_rows), dma(n_rows), dma(n_rows), dma(n_rows), dma(n_rows), dma(n_grp), dma(n_grp),
-        near, near, dma(n_rows // inner), dma(n_rows // inner), near, near,
+        dma(2), both, both, dma(n_grp), dma(n_grp),
+        dma(2), dma(n_rows // inner), dma(n_rows // inner), dma(2),
     ]
     return pl.pallas_call(
         functools.partial(apply_kernel, n_rows, n_grp, slots, chunks),
@@ -550,7 +567,7 @@
         out_specs=(vmem, vmem),
         scratch_shapes=scratch,
         compiler_params=pltpu.CompilerParams(
-            collective_id=0, has_side_effects=True, vmem_limit_bytes=40 * 1024 * 1024),
+            collective_id=0, has_side_effects=True, vmem_limit_bytes=60 * 1024 * 1024),
         name="apply_all",
     )(tiles, tile_row, tile_slot, tile_count, want, omega)
 

time: 182 us -> 161 us (0.88)
  Pallas kernels: 175 us -> 156 us
  local copies, waits for them, and re-layouts: 5.68 us -> 3.34 us
    pallas_call x1, Pallas kernels: 175 us -> 156 us  [per_device(): pl.pallas_call(functools.partial(apply_kernel, n_rows, n_grp, slots, chun...]
    unnamed x12 -> x2, local copies, waits for them, and re-layouts: 5.68 us -> 3.34 us
where the time goes in v4:
time: 161 us
  Pallas kernels  156 us (97%)
  local copies, waits for them, and re-layouts  3.34 us (2%)
    pallas_call x1, Pallas kernels, per_device(): pl.pallas_call(functools.partial(apply_kernel, n_rows, n_grp, slots, chun...  156 us
    unnamed x2, local copies, waits for them, and re-layouts  3.34 us

profile of v4, /device:TPU:1, one launch (start us, length us, event | category | flops | bytes accessed | tf_op | source)
XLA Modules:
  0.0 160.8 jit_solution(12362931737578124492)
XLA Ops:
  1.3 156.2 %apply_all.1 = (f32[256,256]{1,0:T(8,128)}, f32[256,256]{1,0:T(8,128)}) custom-call(bf16[1,1,48,128,128]{4,3,2,1,0:T(8,128)(2,1)} %tiles_ref.1, s32[1,1,48]{2,1,0:T(1,128)} %row_ref.1, s32[1,1,48]{2,1,0:T(1,128)} %slot_ref.1, s32[1,1]{1,0:T(1,128)S(6)} %copy.10.count_ref, s32[1,64]{1,0:T(1,128)} %want_ref.1, bf16[256,256]{1,0:T(8,128)(2,1)} %omega_ref.1), custom_call_target="tpu_custom_call" | custom-call | tf_op jit(solution)/shard_map/apply_all/pallas_call | solution.py:560
  157.5 1.7 %copy.11 = f32[256,256]{1,0:T(8,128)} copy(f32[256,256]{1,0:T(8,128)} %get-tuple-element.4) | data formatting | bytes 524288
  159.1 1.7 %copy.12 = f32[256,256]{1,0:T(8,128)} copy(f32[256,256]{1,0:T(8,128)} %get-tuple-element.5) | data formatting | bytes 524288

commit v5 on v4

--- a/solution.py
+++ b/solution.py
@@ -58,9 +58,9 @@
         pl.semaphore_signal(barrier, inc=1, device_id={"rows": peer(step)}, device_id_type=MESH)
         return carry
 
+    lax.fori_loop(1, n_rows, lambda i, carry: greet(lax.rem(i + n_rows // 4, n_rows - 1) + 1, carry), 0)
     for step in range(1, n_grp):
         pl.semaphore_signal(barrier, inc=1, device_id={"grp": group(step)}, device_id_type=MESH)
-    lax.fori_loop(1, n_rows, greet, 0)
     inner = gram_out.shape[0] // n_grp
     spot = lax.rem(me, inner)
     level = lax.div(me, inner)
@@ -157,7 +157,6 @@
         for step in steps:
             want_copy(step).start()
 
-    each_peer(start_want)
     for step in range(1, n_grp):
         omega_copy(step).start()
         meta_copy(step).start()
@@ -179,6 +178,7 @@
     for c in range(chunks):
         to_right(c).start()
         to_left(c).start()
+    each_peer(start_want)
 
 
     want_part = want_all.at[pl.ds(1, peers)]
@@ -327,27 +327,26 @@
         w_ghosts[h][0] = w_blocks[want_s[0, 0, me]]
         each_peer(start_w)
 
+    def y_copy(step, h):
+        to = group(step)
+        return over_x(
+            y_blocks.at[h, pl.ds(to * owned, owned)], y_in.at[h, step], y_send.at[h, step], y_recv.at[h, step], to)
+
     for h in halves:
         w_trips[h][1]()
         every_chunk(range(n_grp), lambda place, first, count: chunk_y(place, first, count, h))
         for b in range(RBD):
-            y_blocks[b, pl.ds(h * half, half)] = total(LAST_ROW, b, h)
-
-    def y_copy(step):
-        to = group(step)
-        return over_x(
-            y_blocks.at[pl.ds(to * owned, owned)], y_in.at[step], y_send.at[step], y_recv.at[step], to)
-
-    for step in range(1, n_grp):
-        y_copy(step).start()
-    for j in range(owned):
-        y_in[0, j] = y_blocks[grp * owned + j]
-    for step in range(1, n_grp):
-        y_copy(step).wait_recv()
-    for step in range(n_grp):
-        came = group(n_grp - step)
-        for j in range(owned):
-            y_all[pl.ds(pl.multiple_of(came * width, width), width), pl.ds(j * LANES, LANES)] = y_in[step, j]
+            y_blocks[h, b] = total(LAST_ROW, b, h)
+        for step in range(1, n_grp):
+            y_copy(step, h).start()
+    for h in halves:
+        for step in range(1, n_grp):
+            y_copy(step, h).wait_recv()
+        for step in range(n_grp):
+            came = group(n_grp - step)
+            for j in range(owned):
+                value = y_in[h, step, j] if step else y_blocks[h, grp * owned + j]
+                y_all[pl.ds(pl.multiple_of(came * width + h * half, half), half), pl.ds(j * LANES, LANES)] = value
 
     outer = n_rows // inner
     y_value = y_all[...]
@@ -430,7 +429,8 @@
     for step in range(1, n_grp):
         meta_copy(step).wait_send()
         omega_copy(step).wait_send()
-        y_copy(step).wait_send()
+        for h in halves:
+            y_copy(step, h).wait_send()
     wait_others(gram_out, gram_sem.at[0])
     wait_others(gram_all, all_sem.at[0])
     for step in range(1, outer):
@@ -463,15 +463,15 @@
             pivot = spread(columns[0][k][k:k + 1])
             kept = jnp.where(within == k, pivot, kept)
             inverse = 1.0 / pivot
-            ratio = [column[k] * inverse for column in columns]
-            ratio[0] = jnp.where(within > k, ratio[0], 0.0)
+            below = [column[k] for column in columns]
+            below[0] = jnp.where(within > k, below[0], 0.0)
             for j in range(k + 1, EIGHT):
                 entry = spread(columns[0][j][k:k + 1])
                 for r in range(groups - s):
-                    columns[r][j] = columns[r][j] - ratio[r] * entry
+                    columns[r][j] = columns[r][j] - (below[r] * entry) * inverse
             entry = spread(rows[s][k:k + 1])
             for r in range(groups - s):
-                rows[s + r] = rows[s + r] - ratio[r] * entry
+                rows[s + r] = rows[s + r] - (below[r] * entry) * inverse
         pivots.append(kept)
     scaled = jnp.concatenate([rows[r] * lax.rsqrt(pivots[r]) for r in range(groups)], axis=0)
     return scaled[:, size:]
@@ -542,8 +542,8 @@
         pltpu.VMEM((n_rows,) + split[1:], bf16),
         pltpu.VMEM((n_rows,) + split[1:], bf16),
         pltpu.VMEM((2, n_rows) + split[1:], bf16),
-        pltpu.VMEM((RBD,) + block, f32),
-        pltpu.VMEM((n_grp, owned) + block, f32),
+        pltpu.VMEM((2, RBD) + split[1:], f32),
+        pltpu.VMEM((2, n_grp, owned) + split[1:], f32),
         pltpu.VMEM((order, owned * tile), f32),
         pltpu.VMEM((n_grp * inner, some, order), f32),
         pltpu.VMEM((n_grp * inner, some, order), f32),
@@ -554,7 +554,7 @@
         pltpu.VMEM((order, 2 * order), f32),
         dma(5), dma(3), dma(n_grp), dma(n_grp), dma(n_grp), dma(n_grp), dma(2),
         dma(chunks), dma(chunks), dma(chunks), dma(chunks), dma(chunks), dma(chunks),
-        dma(2), both, both, dma(n_grp), dma(n_grp),
+        dma(2), both, both, pltpu.SemaphoreType.DMA((2, n_grp)), pltpu.SemaphoreType.DMA((2, n_grp)),
         dma(2), dma(n_rows // inner), dma(n_rows // inner), dma(2),
     ]
     return pl.pallas_call(

time: 161 us -> 159 us (0.988)
  Pallas kernels: 156 us -> 154 us
    pallas_call x1, Pallas kernels: 156 us -> 154 us  [per_device(): pl.pallas_call(functools.partial(apply_kernel, n_rows, n_grp, slots, chun...]
where the time goes in v5:
time: 159 us; the launch traced here: 158 us
  Pallas kernels  154 us (97%)
  local copies, waits for them, and re-layouts  3.34 us (2%)
    pallas_call x1, Pallas kernels, per_device(): pl.pallas_call(functools.partial(apply_kernel, n_rows, n_grp, slots, chun...  154 us
    unnamed x2, local copies, waits for them, and re-layouts  3.34 us

profile of v5, /device:TPU:1, one launch (start us, length us, event | category | flops | bytes accessed | tf_op | source)
XLA Modules:
  0.0 158.5 jit_solution(9260769720960882953)
XLA Ops:
  1.3 153.8 %apply_all.1 = (f32[256,256]{1,0:T(8,128)}, f32[256,256]{1,0:T(8,128)}) custom-call(bf16[1,1,48,128,128]{4,3,2,1,0:T(8,128)(2,1)} %tiles_ref.1, s32[1,1,48]{2,1,0:T(1,128)} %row_ref.1, s32[1,1,48]{2,1,0:T(1,128)} %slot_ref.1, s32[1,1]{1,0:T(1,128)S(6)} %copy.10.count_ref, s32[1,64]{1,0:T(1,128)} %want_ref.1, bf16[256,256]{1,0:T(8,128)(2,1)} %omega_ref.1), custom_call_target="tpu_custom_call" | custom-call | tf_op jit(solution)/shard_map/apply_all/pallas_call | solution.py:560
  155.1 1.7 %copy.11 = f32[256,256]{1,0:T(8,128)} copy(f32[256,256]{1,0:T(8,128)} %get-tuple-element.4) | data formatting | bytes 524288
  156.8 1.7 %copy.12 = f32[256,256]{1,0:T(8,128)} copy(f32[256,256]{1,0:T(8,128)} %get-tuple-element.5) | data formatting | bytes 524288
